TPU v7x, 128 devices: a whole 4x4x4 slice. The times are simulated.
128 devices in a mesh: wide: 8 (over z, core), narrow: 16 (over x, y).
Axes of the slice: x: 4, y: 4, z: 4, core: 2. Of those that a mesh axis runs over, the one named last changes fastest.
Arguments:
- solution: float32 [512, 256, 128], P(('wide', 'narrow')), may hold values from -6 to 6
- residual: float32 [512, 256, 128], P(('wide', 'narrow')), may hold values from -6 to 6
- direction: float32 [512, 256, 128], P(('wide', 'narrow')), may hold values from -6 to 6
- last_inner: float32 [128], replicated, may hold values from 32768 to 262144
- interface_stiffness_block: bfloat16 [512, 512, 512], P(('wide', 'narrow')), as said below
- cross_conductance: bfloat16 [512, 512, 1152], P(('wide', 'narrow')), may hold values from -0.25 to 0.25
- dirichlet_inverse: bfloat16 [512, 1152, 1152], P(('wide', 'narrow')), as said below
- flux_solve_operator: bfloat16 [512, 512, 512], P(('wide', 'narrow')), as said below
- coarse_shape_functions: bfloat16 [512, 512, 200], P(('wide', 'narrow')), may hold values from -2 to 2
- panels: bfloat16 [512, 200, 200], P(('wide', 'narrow')), as said below
- base_coarse: float32 [8, 256, 256], P('wide'), as said below
- owners: int32 [512, 1], P(('wide', 'narrow')), may hold values from 0 to 7; in each aligned block of 4 rows (0 to 3, 4 to 7, ...) at most 2 rows name the same one
- prim_map: int32 [512, 200], P(('wide', 'narrow')), may hold values from 0 to 255, as said below
- changed: int32 [512], P(('wide', 'narrow')), may hold values 0 or 1
Outputs:
- new_solution: float32 [512, 256, 128], P(('wide', 'narrow'))
- new_residual: float32 [512, 256, 128], P(('wide', 'narrow'))
Inputs may be any that keep to these rules, and one draw needn't show every extreme that they name: `owners`: coarse block of each subdomain in column 0; at most 2 of the 4 subdomains of one device name the same block, and some device reaches 2. `prim_map`: the 200 rows of one subdomain are distinct. `interface_stiffness_block`: each block symmetric positive definite. `dirichlet_inverse`: each block symmetric positive definite. `flux_solve_operator`: each block symmetric positive definite. `panels`: each panel symmetric positive definite. `base_coarse`: each block symmetric positive definite.
All inputs are finite; a program needn't handle non-finite values. No bound on the sum of `changed` on one device may be relied on, other than what follows from the above.
Results may differ from a plain program's by a relative error of at most 0.0014.
Values may be sent and summed in bfloat16 or wider, within the bound.
No kernel may reach another device: no remote copies, remote signals or barrier semaphores. Data moves between devices by JAX's collectives and lax.ppermute only.
A program may use at most 128 MiB of HBM per device.

v0:
```python
import jax
import jax.numpy as jnp
from jax import lax
from jax.sharding import PartitionSpec as P


def shifted(block, axis, distance):
    devices = range(lax.axis_size(axis))
    route = [((i - distance) % len(devices), i) for i in devices]
    return lax.ppermute(block, axis, route)


def local_view(field):
    after = shifted(field[0], "narrow", -1)
    following = jnp.concatenate([field[1:], after[None]], axis=0)
    return jnp.concatenate([field, following], axis=1)


def assemble(local_field):
    face_dofs = local_field.shape[1] // 2
    far_faces = local_field[:, face_dofs:]
    before = shifted(far_faces[-1], "narrow", 1)
    preceding = jnp.concatenate([before[None], far_faces[:-1]], axis=0)
    return local_field[:, :face_dofs] + preceding


def solve_blocks(matrices, right):
    factors = jnp.linalg.cholesky(matrices)
    return jax.vmap(lambda factor, load: jax.scipy.linalg.cho_solve((factor, True), load))(
        factors, right
    )


def dense_terms(blocks, block_rows, owner_index, prim_map, projected, weighted_panels):
    coarse_rhs = (
        jnp.zeros((blocks, block_rows, projected.shape[2]), jnp.float32)
        .at[owner_index[:, None], prim_map]
        .add(projected)
    )
    added = (
        jnp.zeros((blocks, block_rows, block_rows), jnp.float32)
        .at[owner_index[:, None, None], prim_map[:, :, None], prim_map[:, None, :]]
        .add(weighted_panels)
    )
    return (coarse_rhs, added)


def local(
    solution,
    residual,
    direction,
    last_inner,
    interface_stiffness_block,
    cross_conductance,
    dirichlet_inverse,
    flux_solve_operator,
    coarse_shape_functions,
    panels,
    base_coarse,
    owners,
    prim_map,
    changed,
):
    blocks = lax.axis_size("wide")
    block_rows = base_coarse.shape[1]
    owner_index = owners[:, 0]
    subdomain_residual = local_view(residual.astype(jnp.bfloat16))
    projected = jnp.einsum(
        "jok,joz->jkz",
        coarse_shape_functions,
        subdomain_residual,
        preferred_element_type=jnp.float32,
    )
    weighted_panels = panels.astype(jnp.float32) * changed[:, None, None].astype(jnp.float32)
    neumann_part = jnp.einsum(
        "wkn,wnf->wkf", flux_solve_operator, subdomain_residual, preferred_element_type=jnp.float32
    )
    coarse_rhs, added = dense_terms(
        blocks, block_rows, owner_index, prim_map, projected, weighted_panels
    )
    flags = (
        (jnp.arange(blocks, dtype=jnp.int32) == lax.axis_index("wide"))
        & (lax.axis_index("narrow") == 0)
    ).astype(jnp.float32)
    added = added + flags[:, None, None] * base_coarse
    total_rhs, total_matrix = lax.psum((coarse_rhs, added), ("wide", "narrow"))
    coarse_solution = solve_blocks(total_matrix, total_rhs).astype(jnp.bfloat16)
    selected_entries = coarse_solution[owner_index[:, None], prim_map]
    precond_local = neumann_part + jnp.einsum(
        "ney,nyx->nex", coarse_shape_functions, selected_entries, preferred_element_type=jnp.float32
    )
    precond = 0.5 * assemble(precond_local)
    inner = lax.psum(jnp.sum(residual * precond, axis=(0, 1)), ("wide", "narrow"))
    search = precond + inner / last_inner * direction
    local_search_vector = local_view(search.astype(jnp.bfloat16))
    enclosed_source_vector = jnp.einsum(
        "wnz,wnf->wzf", cross_conductance, local_search_vector, preferred_element_type=jnp.float32
    ).astype(jnp.bfloat16)
    enclosed_heat_values = jnp.einsum(
        "sij,sjr->sir",
        dirichlet_inverse,
        enclosed_source_vector,
        preferred_element_type=jnp.float32,
    ).astype(jnp.bfloat16)
    image_local = jnp.einsum(
        "wkn,wnf->wkf",
        interface_stiffness_block,
        local_search_vector,
        preferred_element_type=jnp.float32,
    ) - jnp.einsum(
        "mpj,mjt->mpt", cross_conductance, enclosed_heat_values, preferred_element_type=jnp.float32
    )
    image = assemble(image_local)
    curvature = lax.psum(jnp.sum(search * image, axis=(0, 1)), ("wide", "narrow"))
    step_size = inner / curvature
    return (solution + step_size * search, residual - step_size * image)


def solution(mesh):
    in_specs = (
        P(("wide", "narrow"), None, None),
        P(("wide", "narrow"), None, None),
        P(("wide", "narrow"), None, None),
        P(),
        P(("wide", "narrow"), None, None),
        P(("wide", "narrow"), None, None),
        P(("wide", "narrow"), None, None),
        P(("wide", "narrow"), None, None),
        P(("wide", "narrow"), None, None),
        P(("wide", "narrow"), None, None),
        P("wide", None, None),
        P(("wide", "narrow"), None),
        P(("wide", "narrow"), None),
        P(("wide", "narrow")),
    )
    out_specs = (P(("wide", "narrow"), None, None), P(("wide", "narrow"), None, None))
    return jax.shard_map(local, mesh=mesh, in_specs=in_specs, out_specs=out_specs, check_vma=False)
```

profile of v0, /device:TPU:1, one launch (start us, length us, event | category | flops | bytes accessed | tf_op | source)
XLA Modules:
  0.0 2007.0 jit_solution(12850405900955359618)
XLA Ops:
  10.1 5.8 collective-permute-start
  26.2 4.0 copy.87
  34.3 1102.9 %scatter_fusion.1 = f32[524288]{0:T(1024)} fusion(f32[524288]{0:T(1024)} %bitcast.91, s32[160000]{0:T(1024)S(1)} %reshape.109, f32[160000]{0:T(1024)S(1)} %reshape.111), kind=kCustom, calls=%fused_computation.2 | custom fusion | flops 160000 | bytes 2560000
  1137.2 2.9 reshape.75
  1140.1 3.0 copy.60
  1145.2 51.9 %scatter_fusion = f32[8,256,128]{2,1,0:T(8,128)S(1)} fusion(f32[8,256,128]{2,1,0:T(8,128)S(1)} %broadcast_in_dim.64, s32[800]{0:T(1024)S(1)} %copy-done.1, f32[800,128]{1,0:T(8,128)} %bitcast.94), kind=kCustom, calls=%fused_computation.1 | custom fusion | flops 102400 | bytes 1235200 | tf_op jit(solution)/shard_map/scatter-add | solution.py:38
  1198.3 151.2 %all-reduce.4.cloned.1.call-done = (f32[8,256,128]{2,1,0:T(8,128)}, f32[8,256,256]{1,2,0:T(8,128)}) async-done(((f32[8,256,128]{2,1,0:T(8,128)}, f32[8,256,256]{1,2,0:T(8,128)}), (f32[8,256,128]{2,1,0:T(8,128)}, f32[8,256,256]{1,2,0:T(8,128)})) %all-reduce.4.cloned.1.call-update) | async-done | bytes 3145744 | tf_op jit(solution)/shard_map/psum | solution.py:86
  1349.5 2.9 copy.61
  1356.3 93.8 %custom-call.20 = f32[8,128,128]{2,1,0:T(8,128)S(1)} custom-call(f32[8,128,128]{2,1,0:T(8,128)S(1)} %cholesky.119), custom_call_target="Cholesky" | custom-call | tf_op jit(solution)/shard_map/jit(cholesky)/cholesky | solution.py:28
  1451.7 79.2 %custom-call.21 = f32[8,1,128,128]{2,3,1,0:T(8,128)} custom-call(f32[8,1,128,128]{3,2,1,0:T(8,128)S(1)} %select_bitcast_fusion), custom_call_target="InvertDiagBlocksLowerTriangular" | custom-call | tf_op jit(solution)/shard_map/jit(cholesky)/cholesky | solution.py:28
  1533.6 3.1 convolution_subtract_fusion.3
  1536.6 94.7 %custom-call.22 = f32[8,128,128]{2,1,0:T(8,128)S(1)} custom-call(f32[8,128,128]{2,1,0:T(8,128)} %convolution_subtract_fusion.3), custom_call_target="Cholesky" | custom-call | tf_op jit(solution)/shard_map/jit(cholesky)/cholesky | solution.py:28
  1632.4 3.3 select_select_fusion
  1635.7 8.0 while.1
  1636.3 3.5 bitcast_dynamic-update-slice_fusion.2
  1640.4 3.3 bitcast_dynamic-update-slice_fusion.2
  1643.7 158.0 %custom-call.23 = f32[8,2,128,128]{2,3,1,0:T(8,128)S(1)} custom-call(f32[8,2,128,128]{3,2,1,0:T(8,128)} %bitcast.100), custom_call_target="InvertDiagBlocksLowerTriangular" | custom-call | tf_op jit(solution)/shard_map/vmap(jit(_cho_solve))/triangular_solve | solution.py:29
  1810.1 9.4 gather_fusion
  1827.0 3.8 collective-permute-done.1
  1832.1 65.5 %psum.30 = f32[128]{0:T(128)S(1)} all-reduce(f32[128]{0:T(128)S(1)} %multiply_reduce_fusion.1), channel_id=1, replica_groups=mesh['wide'=8,'narrow'=16] {'wide','narrow'}, use_global_device_ids=true, to_apply=%region_9.10 | all-reduce | flops 128 | bytes 1024 | tf_op jit(solution)/shard_map/psum | solution.py:93
  1902.8 10.5 convolution_convert_fusion
  1913.3 4.5 fusion.34
  1923.3 4.7 collective-permute-done.3
  1929.3 64.2 %psum.31 = f32[128]{0:T(128)S(1)} all-reduce(f32[128]{0:T(128)S(1)} %multiply_reduce_fusion), channel_id=1, replica_groups=mesh['wide'=8,'narrow'=16] {'wide','narrow'}, use_global_device_ids=true, to_apply=%region_11.12 | all-reduce | flops 128 | bytes 1024 | tf_op jit(solution)/shard_map/psum | solution.py:114
  (125 shorter events, 66.4 us)
Async XLA Ops:
  7.2 1813.8 %copy-start = (bf16[4,512,512]{2,1,0:T(8,128)(2,1)S(1)}, bf16[4,512,512]{2,1,0:T(8,128)(2,1)}, u32[]{:S(2)}) copy-start(bf16[4,512,512]{2,1,0:T(8,128)(2,1)} %param.21) | copy-start | bytes 6291460
  7.2 10.4 copy-start.21
  7.2 1342.3 %all-reduce.4.cloned.1.call-start = ((), (), s32[]{:S(2)}) async-start(), calls=%async_computation | async-start | bytes 6291456 | tf_op jit(solution)/shard_map/psum | solution.py:86
  8.6 10.3 copy-start.3
  10.1 1133.1 %collective-permute-start = (bf16[256,128]{0,1:T(8,128)(2,1)}, bf16[256,128]{0,1:T(8,128)(2,1)}, u32[]{:S(2)}, u32[]{:S(2)}) collective-permute-start(bf16[256,128]{0,1:T(8,128)(2,1)} %slice_bitcast_fusion.9), channel_id=1, source_target_pairs={{1,0},{2,1},{3,2},{4,3},{5,4},{6,5},{7,6},{8,7},{9,8},{10,9},{11,1... | collective-permute-start | bytes 196616 | tf_op jit(solution)/shard_map/ppermute | solution.py:10
  17.3 1.6 copy-start.22
  19.5 2.6 copy-start.14
  19.5 3.6 copy-start.18
  22.2 2.1 copy-start.19
  22.2 2.7 copy-start.10
  1140.1 3.0 copy-start.11
  1140.1 3.1 copy-start.15
  1140.1 3.1 copy-start.16
  1143.2 2.1 copy-start.1
  1355.0 1.3 copy-start.7
  1810.1 10.9 copy-start.17
  1823.6 7.2 copy-start.4
  1823.6 73.9 %copy-start.24 = (f32[128]{0:T(128)S(1)}, f32[128]{0:T(128)}, u32[]{:S(2)}) copy-start(f32[128]{0:T(128)} %param.17) | copy-start | bytes 1540
  1823.6 7.2 collective-permute-start.1
  1827.0 3.8 copy-start.8
  1899.0 3.7 collective-permute-start.2
  1913.3 4.5 copy-start.12
  1913.3 4.5 copy-start.13
  1920.2 7.8 collective-permute-start.3
  (6 other events, 5.4 us)
Sparse Core Ops, SparseCore 0:
  1198.3 151.1 all-reduce.3
where the time goes:
time: 2020 us; the launch traced here: 2010 us
  other arithmetic  1600 us (79%)
  waiting for transfers between devices  160 us (8%)
  blocking collectives  130 us (6%)
  local copies, waits for them, and re-layouts  56.7 us (3%)
  matrix products  35 us (2%)
    unnamed x5, other arithmetic  1110 us
    another operation x9, other arithmetic, solve_blocks(): factors = jnp.linalg.cholesky(matrices)  269 us
    another operation x5, other arithmetic, solve_blocks(): jax.scipy.linalg.cho_solve((factor, True), load)  161 us
    psum x1, waiting for transfers between devices, local(): total_rhs, total_matrix = lax.psum((coarse_rhs, added), ('wide', 'narrow'))  151 us
    psum x1, blocking collectives, local(): lax.psum(jnp.sum(residual * precond, axis=(0, 1)), ('wide', 'narrow'))  65.5 us
    psum x1, blocking collectives, local(): lax.psum(jnp.sum(search * image, axis=(0, 1)), ('wide', 'narrow'))  64.2 us
    scatter-add x1, other arithmetic, dense_terms(): coarse_rhs = jnp.zeros((blocks, block_rows, projected.shape[2]), jnp.floa...  51.9 us
  transfers between devices with their start and end apart: 5, of which 4 were waited for; matrix products, arithmetic and copies ran while one was open for 56% of the time, Pallas kernels for 0%

commit v1 on v0

v1 whole, which is shorter than its diff:
```python
import jax
import jax.numpy as jnp
from jax import lax
from jax.experimental import pallas as pl
from jax.experimental.pallas import tpu as pltpu
from jax.sharding import Mesh, PartitionSpec as P

F32 = jnp.float32
BF16 = jnp.bfloat16
NN = (((1,), (0,)), ((), ()))
NT = (((1,), (1,)), ((), ()))
TN = (((0,), (0,)), ((), ()))
LIMIT = 24 * 1024 * 1024


def dot(a, b, dims=NN, precision=None):
    return lax.dot_general(a, b, dims, precision=precision, preferred_element_type=F32)


def smem():
    return pl.BlockSpec(memory_space=pltpu.SMEM)


def whole(shape):
    return pl.BlockSpec(shape, lambda *_: (0,) * len(shape))


def params(*semantics):
    return pltpu.CompilerParams(vmem_limit_bytes=LIMIT)


def place_kernel(own, chg, core, pm, basis, panel, res, keep, send, spread):
    s = pl.program_id(0)
    co = spread.shape[2]
    half = co // 2
    face = res.shape[1]

    @pl.when(s == 0)
    def _():
        keep[...] = jnp.zeros_like(keep)
        send[...] = jnp.zeros_like(send)

    rows = lax.broadcasted_iota(jnp.int32, (co, pm.shape[2]), 0)
    select = (rows == pm[0]).astype(F32).astype(BF16)
    wide_basis = dot(basis[0], select, NT).astype(BF16)
    spread[0] = wide_basis
    placed = dot(dot(select, panel[0]).astype(BF16), select, NT) * chg[s].astype(F32)
    last = pl.num_programs(0) - 1
    here = res[s].astype(BF16)
    there = res[jnp.minimum(s + 1, last)].astype(BF16)
    rhs = dot(wide_basis[:face], here, TN)
    rhs += jnp.where(s < last, dot(wide_basis[face:], there, TN), 0.0)
    owner = own[s]
    place = owner >> 1
    other = (owner & 1) != core[0]

    def add(to):
        to[place, 0:half] += placed[:half, :half]
        to[place, half:co] += placed[half:, :half]
        to[place, co : co + half] += placed[half:, half:]
        to[place, co + half :] += rhs

    @pl.when(other)
    def _():
        add(send)

    @pl.when(jnp.logical_not(other))
    def _():
        add(keep)


def place_panels(own, chg, core, prim_map, basis, panels, residual, groups):
    subs, nb, npr = basis.shape
    co = 2 * residual.shape[2]
    rows = 3 * (co // 2) + co
    packed = (groups, rows, co // 2)
    return pl.pallas_call(
        place_kernel,
        grid=(subs,),
        in_specs=[
            smem(),
            smem(),
            smem(),
            pl.BlockSpec((1, 1, npr), lambda s: (s, 0, 0)),
            pl.BlockSpec((1, nb, npr), lambda s: (s, 0, 0)),
            pl.BlockSpec((1, npr, npr), lambda s: (s, 0, 0)),
            whole(residual.shape),
        ],
        out_specs=[whole(packed), whole(packed), pl.BlockSpec((1, nb, co), lambda s: (s, 0, 0))],
        out_shape=[
            jax.ShapeDtypeStruct(packed, F32),
            jax.ShapeDtypeStruct(packed, F32),
            jax.ShapeDtypeStruct((subs, nb, co), BF16),
        ],
        compiler_params=params(),
        cost_estimate=pl.CostEstimate(flops=10**9, bytes_accessed=6 * 10**6, transcendentals=0),
        name="place_panels",
    )(own, chg, core, prim_map, basis, panels, residual)


def halo_kernel(own, core, spread, halo, keep_in, send_in, keep, send, held, sem):
    del keep_in, send_in
    owner = own[own.shape[0] - 1]
    place = owner >> 1
    other = (owner & 1) != core[0]
    rows = held.shape[0]

    def add(to):
        part = to.at[place, pl.ds(to.shape[1] - rows, rows)]
        fetch = pltpu.make_async_copy(part, held, sem)
        fetch.start()
        value = dot(spread[0], halo[...], TN)
        fetch.wait()
        held[...] += value
        put = pltpu.make_async_copy(held, part, sem)
        put.start()
        put.wait()

    @pl.when(other)
    def _():
        add(send)

    @pl.when(jnp.logical_not(other))
    def _():
        add(keep)


def add_halo(own, core, spread, halo, keep, send):
    subs, nb, co = spread.shape
    hbm = pl.BlockSpec(memory_space=pl.ANY)
    return pl.pallas_call(
        halo_kernel,
        grid=(1,),
        in_specs=[
            smem(),
            smem(),
            pl.BlockSpec((1, nb // 2, co), lambda _: (subs - 1, 1, 0)),
            whole(halo.shape),
            hbm,
            hbm,
        ],
        out_specs=[hbm, hbm],
        out_shape=[jax.ShapeDtypeStruct(keep.shape, F32), jax.ShapeDtypeStruct(send.shape, F32)],
        input_output_aliases={4: 0, 5: 1},
        scratch_shapes=[pltpu.VMEM((co, halo.shape[1]), F32), pltpu.SemaphoreType.DMA],
        compiler_params=params(),
        name="add_halo",
    )(own, core, spread, halo, keep, send)


def inverse(matrix):
    n = matrix.shape[0]
    lanes = lax.broadcasted_iota(jnp.int32, (8, n), 1)
    subl = lax.broadcasted_iota(jnp.int32, (8, n), 0)
    tiles = tuple(matrix[8 * i : 8 * i + 8] for i in range(n // 8))

    def group(_, tiles):
        tiles = list(tiles)
        for j in range(8):
            pivot_row = tiles[0][j : j + 1, :]
            scale = 1.0 / pivot_row[:, j : j + 1]
            row = jnp.where(lanes[:1] == j, scale, pivot_row * scale)
            for i, tile in enumerate(tiles):
                new = jnp.where(lanes == j, 0.0, tile) - tile[:, j : j + 1] * row
                if i == 0:
                    new = jnp.where(subl == j, row, new)
                tiles[i] = new
        return tuple(pltpu.roll(tile, n - 8, 1) for tile in tiles[1:] + tiles[:1])

    return jnp.concatenate(lax.fori_loop(0, n // 8, group, tiles), axis=0)


def solve_kernel(packed, base, out):
    co = out.shape[0]
    half = co // 2
    high = lax.Precision.HIGHEST
    a11 = packed[0:half] + base[0, :half, :half]
    a21 = packed[half:co] + base[0, half:, :half]
    a22 = packed[co : co + half] + base[0, half:, half:]
    b1 = packed[co + half : 2 * co]
    b2 = packed[2 * co :]
    inv1 = inverse(a11)
    carry = dot(a21, inv1, NN, high)
    inv2 = inverse(a22 - dot(carry, a21, NT, high))
    x2 = dot(inv2, b2 - dot(carry, b1, NN, high), NN, high)
    x1 = dot(inv1, b1, NN, high) - dot(carry, x2, TN, high)
    out[:half] = x1.astype(BF16)
    out[half:] = x2.astype(BF16)


def solve_block(packed, base):
    co = base.shape[1]
    return pl.pallas_call(
        solve_kernel,
        out_shape=jax.ShapeDtypeStruct((co, packed.shape[1]), BF16),
        compiler_params=params(),
        name="solve_block",
    )(packed, base)


def neumann_kernel(neumann, res, halo, out):
    s = pl.program_id(0)
    last = pl.num_programs(0) - 1
    here = res[s].astype(BF16)
    there = jnp.where(s < last, res[jnp.minimum(s + 1, last)], halo[...].astype(F32)).astype(BF16)
    out[0] = 0.5 * dot(neumann[0], jnp.concatenate([here, there], axis=0))


def neumann_half(neumann, residual, halo):
    subs, nb, _ = neumann.shape
    rhs = residual.shape[2]
    return pl.pallas_call(
        neumann_kernel,
        grid=(subs,),
        in_specs=[
            pl.BlockSpec((1, nb, nb), lambda s: (s, 0, 0)),
            whole(residual.shape),
            whole(halo.shape),
        ],
        out_specs=pl.BlockSpec((1, nb, rhs), lambda s: (s, 0, 0)),
        out_shape=jax.ShapeDtypeStruct((subs, nb, rhs), F32),
        compiler_params=params(),
        cost_estimate=pl.CostEstimate(
            flops=2 * subs * nb * nb * rhs, bytes_accessed=4 * 10**6, transcendentals=0
        ),
        name="neumann_half",
    )(neumann, residual, halo)


def coarse_kernel(own, spread, solved, part, out):
    s = pl.program_id(0)
    out[0] = part[0] + 0.5 * dot(spread[0], solved[own[s]])


def coarse_part(own, spread, solved, part):
    subs, nb, co = spread.shape
    rhs = solved.shape[2]
    return pl.pallas_call(
        coarse_kernel,
        grid=(subs,),
        in_specs=[
            smem(),
            pl.BlockSpec((1, nb, co), lambda s: (s, 0, 0)),
            whole(solved.shape),
            pl.BlockSpec((1, nb, rhs), lambda s: (s, 0, 0)),
        ],
        out_specs=pl.BlockSpec((1, nb, rhs), lambda s: (s, 0, 0)),
        out_shape=jax.ShapeDtypeStruct((subs, nb, rhs), F32),
        compiler_params=params(),
        name="coarse_part",
    )(own, spread, solved, part)


def action(stiffness, coupling, interior, field):
    load = dot(coupling, field, TN).astype(BF16)
    inside = dot(interior, load).astype(BF16)
    return dot(stiffness, field) - dot(coupling, inside)


def operators(nb, ni, place):
    return [
        pl.BlockSpec((1, nb, nb), place),
        pl.BlockSpec((1, nb, ni), place),
        pl.BlockSpec((1, ni, ni), place),
    ]


def cost(steps, nb, ni, rhs):
    return pl.CostEstimate(
        flops=2 * steps * rhs * (nb * nb + 2 * nb * ni + ni * ni),
        bytes_accessed=2 * steps * (nb * nb + nb * ni + ni * ni),
        transcendentals=0,
    )


def direction_kernel(stiffness, coupling, interior, direction, halo, out):
    s = pl.program_id(0)
    last = pl.num_programs(0) - 1
    there = jnp.where(s < last, direction[jnp.minimum(s + 1, last)], halo[...])
    field = jnp.concatenate([direction[s], there], axis=0).astype(BF16)
    out[0] = action(stiffness[0], coupling[0], interior[0], field)


def direction_action(stiffness, coupling, interior, direction, halo):
    subs, nb, ni = coupling.shape
    rhs = direction.shape[2]
    return pl.pallas_call(
        direction_kernel,
        grid=(subs,),
        in_specs=operators(nb, ni, lambda s: (s, 0, 0)) + [whole(direction.shape), whole(halo.shape)],
        out_specs=pl.BlockSpec((1, nb, rhs), lambda s: (s, 0, 0)),
        out_shape=jax.ShapeDtypeStruct((subs, nb, rhs), F32),
        compiler_params=params(),
        cost_estimate=cost(subs, nb, ni, rhs),
        name="direction_action",
    )(stiffness, coupling, interior, direction, halo)


def column_sum(value):
    return jnp.sum(value, axis=0, keepdims=True)


def products(out, sums, image, own_p, far_p, own_d, far_d, own_r, moved_d, first, earlier):
    face = own_p.shape[0]
    out[0] = image
    parts = jnp.concatenate(
        [
            column_sum(own_r * own_p),
            column_sum(own_p * image[:face] + far_p * image[face:]),
            column_sum(own_p * moved_d[:face] + far_p * moved_d[face:])
            + column_sum(own_d * image[:face] + far_d * image[face:]),
            column_sum(own_d * moved_d[:face] + far_d * moved_d[face:]),
        ],
        axis=0,
    )

    @pl.when(first)
    def _():
        sums[...] = earlier + parts

    @pl.when(jnp.logical_not(first))
    def _():
        sums[...] += parts


def inner_kernel(stiffness, coupling, interior, pre, direction, residual, moved, out, sums):
    i = pl.program_id(0)
    s = i + 1
    face = direction.shape[1]
    own_p = pre[s, :face] + pre[s - 1, face:]
    far_p = pre[s + 1, :face] + pre[s, face:]
    field = jnp.concatenate([own_p, far_p], axis=0).astype(BF16)
    image = action(stiffness[0], coupling[0], interior[0], field)
    products(
        out, sums, image, own_p, far_p, direction[s], direction[s + 1], residual[s], moved[s], i == 0, 0.0
    )


def outer_kernel(
    stiffness,
    coupling,
    interior,
    pre,
    from_prev,
    from_next,
    direction,
    direction_halo,
    residual,
    moved,
    earlier,
    out,
    sums,
):
    i = pl.program_id(0)
    last = direction.shape[0] - 1
    s = i * last
    near = jnp.minimum(s + 1, last)
    behind = jnp.maximum(s - 1, 0)
    face = direction.shape[1]
    own_p = pre[s, :face] + jnp.where(i == 0, from_prev[...], pre[behind, face:])
    far_p = pre[s, face:] + jnp.where(i == 0, pre[near, :face], from_next[...])
    far_d = jnp.where(i == 0, direction[near], direction_halo[...])
    field = jnp.concatenate([own_p, far_p], axis=0).astype(BF16)
    image = action(stiffness[0], coupling[0], interior[0], field)
    products(
        out, sums, image, own_p, far_p, direction[s], far_d, residual[s], moved[s], i == 0, earlier[...]
    )


def search_action(kernel, place, steps, stiffness, coupling, interior, *rest):
    _, nb, ni = coupling.shape
    rhs = rest[0].shape[2]
    return pl.pallas_call(
        kernel,
        grid=(steps,),
        in_specs=operators(nb, ni, place) + [whole(x.shape) for x in rest],
        out_specs=[pl.BlockSpec((1, nb, rhs), lambda i: (i, 0, 0)), whole((4, rhs))],
        out_shape=[
            jax.ShapeDtypeStruct((steps, nb, rhs), F32),
            jax.ShapeDtypeStruct((4, rhs), F32),
        ],
        compiler_params=params(),
        cost_estimate=cost(steps, nb, ni, rhs),
        name="search_action",
    )(stiffness, coupling, interior, *rest)


def update_kernel(
    sums, last_inner, pre, from_prev, outer, inside, moved, far, direction, residual, solution, new_sol, new_res
):
    total = jnp.sum(sums[...], axis=0)
    inner = total[0:1]
    beta = inner / last_inner[...]
    curvature = total[1:2] + beta * (total[2:3] + beta * total[3:4])
    step = inner / curvature
    face = direction.shape[1]
    last = direction.shape[0] - 1

    def part(s):
        return outer[0] if s == 0 else outer[1] if s == last else inside[s - 1]

    for s in range(last + 1):
        if s == 0:
            p = pre[s, :face] + from_prev[...]
            image = part(s)[:face] + far[0] + beta * (moved[s, :face] + far[1])
        else:
            p = pre[s, :face] + pre[s - 1, face:]
            image = part(s)[:face] + part(s - 1)[face:] + beta * (moved[s, :face] + moved[s - 1, face:])
        search = p + beta * direction[s]
        new_sol[s] = solution[s] + step * search
        new_res[s] = residual[s] - step * image


def update(*args):
    shape = jax.ShapeDtypeStruct(args[-1].shape, F32)
    return pl.pallas_call(
        update_kernel, out_shape=[shape, shape], compiler_params=params(), name="update"
    )(*args)


def local(
    solution,
    residual,
    direction,
    last_inner,
    stiffness,
    coupling,
    interior,
    neumann,
    basis,
    panels,
    base_coarse,
    owners,
    prim_map,
    changed,
):
    groups = lax.axis_size("z")
    pieces = lax.axis_size("narrow")
    devices = groups * 2 * pieces
    face, rhs = residual.shape[1:]
    forward = [(i, (i + 1) % pieces) for i in range(pieces)]
    back = [((i + 1) % pieces, i) for i in range(pieces)]
    own = owners[:, 0]
    core = lax.axis_index("core")
    core_ref = core.astype(jnp.int32).reshape(1)

    halo = lax.ppermute(residual[0].astype(BF16), "narrow", back)
    keep, send, spread = place_panels(
        own, changed, core_ref, prim_map[:, None, :], basis, panels, residual, groups
    )
    keep, send = add_halo(own, core_ref, spread, halo, keep, send)
    face_d, _ = lax.optimization_barrier((direction[0], halo))
    direction_halo = lax.ppermute(face_d, "narrow", back)
    mine = keep + lax.ppermute(send, "core", [(0, 1), (1, 0)])
    rows = mine.shape[1] // pieces
    parts = lax.all_to_all(
        mine.reshape(groups * pieces, rows, rhs), ("z", "narrow"), 0, 0, tiled=True
    )
    piece = jnp.sum(parts, axis=0)
    packed = lax.all_to_all(
        jnp.broadcast_to(piece[None], (pieces,) + piece.shape), "narrow", 0, 0, tiled=True
    )
    solved = solve_block(packed.reshape(pieces * rows, rhs), base_coarse)

    turns = [lax.ppermute(solved, "z", [(i, (i + d) % groups) for i in range(groups)]) for d in range(1, groups)]
    ring = jnp.stack([solved] + turns)
    twin = lax.ppermute(ring, "core", [(0, 1), (1, 0)])
    pairs = jnp.stack([ring, twin]).reshape((2 * groups,) + solved.shape)
    z = lax.axis_index("z")
    where = ((own & 1) != core) * groups + (z - (own >> 1)) % groups

    part = neumann_half(neumann, residual, halo)
    moved = direction_action(stiffness, coupling, interior, direction, direction_halo)
    pre = coarse_part(where.astype(jnp.int32), spread, pairs, part)
    from_prev = lax.ppermute(pre[-1, face:], "narrow", forward)
    from_next = lax.ppermute(pre[0, :face], "narrow", back)
    inside, sums = search_action(
        inner_kernel, lambda i: (i + 1, 0, 0), 2, stiffness, coupling, interior, pre, direction, residual, moved
    )
    last = residual.shape[0] - 1
    outer, sums = search_action(
        outer_kernel,
        lambda i: (last * i, 0, 0),
        2,
        stiffness,
        coupling,
        interior,
        pre,
        from_prev,
        from_next,
        direction,
        direction_halo,
        residual,
        moved,
        sums,
    )
    far = lax.ppermute(jnp.stack([outer[-1, face:], moved[-1, face:]]), "narrow", forward)
    sums = lax.all_to_all(
        jnp.broadcast_to(sums[None], (devices,) + sums.shape), ("z", "core", "narrow"), 0, 0, tiled=True
    )
    return tuple(
        update(
            sums,
            last_inner[None],
            pre,
            from_prev,
            outer,
            inside,
            moved,
            far,
            direction,
            residual,
            solution,
        )
    )


def solution(mesh):
    wide, narrow = mesh.devices.shape
    finer = Mesh(mesh.devices.reshape(wide // 2, 2, narrow), ("z", "core", "narrow"))
    split = ("z", "core", "narrow")
    in_specs = (
        P(split, None, None),
        P(split, None, None),
        P(split, None, None),
        P(),
        P(split, None, None),
        P(split, None, None),
        P(split, None, None),
        P(split, None, None),
        P(split, None, None),
        P(split, None, None),
        P(("z", "core"), None, None),
        P(split, None),
        P(split, None),
        P(split),
    )
    out_specs = (P(split, None, None), P(split, None, None))
    return jax.shard_map(local, mesh=finer, in_specs=in_specs, out_specs=out_specs, check_vma=False)
```

time: 2020 us -> 149 us (0.07)
  other arithmetic: 1600 us -> 1.83 us
  waiting for transfers between devices: 160 us -> 10.3 us
  blocking collectives: 130 us -> 48.2 us
  Pallas kernels: 0 us -> 51.3 us
  local copies, waits for them, and re-layouts: 56.7 us -> 11.3 us
  matrix products: 35 us -> 0 us
    unnamed x5 -> x0, other arithmetic: 1110 us -> none
    another operation x14 -> x3, other arithmetic: 430 us -> 0.12 us  [the longest x2 0.1 us: local(): pairs = jnp.stack([ring, twin]).reshape((2 * groups,) + solved.shape)]
    psum x1 -> x0, waiting for transfers between devices: 151 us -> none  [local(): total_rhs, total_matrix = lax.psum((coarse_rhs, added), ('wide', 'narrow'))]
    psum x2 -> x0, blocking collectives: 130 us -> none  [the longest x1 65.5 us: local(): lax.psum(jnp.sum(residual * precond, axis=(0, 1)), ('wide', 'narrow'))]
    scatter-add x1 -> x0, other arithmetic: 51.9 us -> none  [dense_terms(): coarse_rhs = jnp.zeros((blocks, block_rows, projected.shape[2]), jnp.floa...]
    pallas_call x0 -> x9, Pallas kernels: none -> 51.3 us  [the longest x1 25.1 us: solve_block(): pl.pallas_call(solve_kernel, out_shape=jax.ShapeDtypeStruct((co, packed.s...]
    all_to_all x0 -> x2, blocking collectives: none -> 48.2 us  [the longest x1 28.3 us: local(): lax.all_to_all(mine.reshape(groups * pieces, rows, rhs), ('z', 'narrow'),...]
    dot_general x6 -> x0, matrix products: 20.9 us -> none  [the longest x1 10.5 us: local(): jnp.einsum('sij,sjr->sir', dirichlet_inverse, enclosed_source_vector, pre...]
  transfers between devices with their start and end apart: 5 -> 11, of which waited for: 4 -> 2; matrix products, arithmetic and copies ran while one was open for 56% -> 1% of each run, Pallas kernels for 0% -> 12%
where the time goes in v1:
time: 149 us; the launch traced here: 148 us
  Pallas kernels  51.3 us (34%)
  blocking collectives  48.2 us (32%)
  starting transfers between devices  24.1 us (16%)
  local copies, waits for them, and re-layouts  11.3 us (8%)
  waiting for transfers between devices  10.3 us (7%)
  other arithmetic  1.83 us (1%)
    all_to_all x1, blocking collectives, local(): lax.all_to_all(mine.reshape(groups * pieces, rows, rhs), ('z', 'narrow'),...  28.3 us
    pallas_call x1, Pallas kernels, solve_block(): pl.pallas_call(solve_kernel, out_shape=jax.ShapeDtypeStruct((co, packed.s...  25.1 us
    all_to_all x1, blocking collectives, local(): lax.all_to_all(jnp.broadcast_to(sums[None], (devices,) + sums.shape), ('z...  19.9 us
    unnamed x31, local copies, waits for them, and re-layouts  9.43 us
    pallas_call x2, Pallas kernels, search_action(): pl.pallas_call(kernel, grid=(steps,), in_specs=operators(nb, ni, place) +...  8.92 us
    pallas_call x1, Pallas kernels, direction_action(): pl.pallas_call(direction_kernel, grid=(subs,), in_specs=operators(nb, ni,...  8.76 us
    all_to_all x1, waiting for transfers between devices, local(): lax.all_to_all(jnp.broadcast_to(piece[None], (pieces,) + piece.shape), 'n...  7.64 us
    ppermute x1, starting transfers between devices, local(): halo = lax.ppermute(residual[0].astype(BF16), 'narrow', back)  5.76 us
  transfers between devices with their start and end apart: 11, of which 2 were waited for; matrix products, arithmetic and copies ran while one was open for 1% of the time, Pallas kernels for 12%

profile of v1, /device:TPU:1, one launch (start us, length us, event | category | flops | bytes accessed | tf_op | source)
XLA Modules:
  0.0 148.1 jit_solution(8676325799122263523)
XLA Ops:
  1.7 5.8 %collective-permute-start = (bf16[256,128]{1,0:T(8,128)(2,1)S(1)}, bf16[256,128]{1,0:T(8,128)(2,1)S(1)}, u32[]{:S(2)}, u32[]{:S(2)}) collective-permute-start(bf16[256,128]{1,0:T(8,128)(2,1)S(1)} %fusion), channel_id=1, source_target_pairs={{1,0},{2,1},{3,2},{4,3},{5,4},{6,5},{7,6},{8,7},{9,8},{10,9},{11,1... | collective-permute-start | bytes 196616 | tf_op jit(solution)/shard_map/ppermute | solution.py:447
  7.4 1.4 copy.18.basis
  8.9 3.3 %place_panels.1 = (f32[4,640,128]{2,1,0:T(8,128)S(1)}, f32[4,640,128]{2,1,0:T(8,128)S(1)}, bf16[4,512,256]{2,1,0:T(8,128)(2,1)S(1)}) custom-call(s32[4]{0:T(128)S(1)} %bitcast.25, s32[4]{0:T(128)S(1)} %copy-done.13, s32[1]{0:T(128)} %bitcast.1.core, s32[4,1,200]{2,1,0:T(1,128)S(1)} %broadcast_in_dim.8.pm, bf16[4,512,200]{2,1,0:T(8,128)(2,1)S(1)} %copy.18.basis, ...), custom_call_target="tpu_custom_call" | custom-call | flops 1000000000 | bytes 6000000 | tf_op jit(solution)/shard_map/place_panels/pallas_call | solution.py:77
  12.2 1.1 add_halo.1
  14.4 2.7 %collective-permute-done.1 = f32[4,640,128]{2,1,0:T(8,128)S(1)} collective-permute-done((f32[4,640,128]{2,1,0:T(8,128)S(1)}, f32[4,640,128]{2,1,0:T(8,128)S(1)}, u32[]{:S(2)}, u32[]{:S(2)}) %collective-permute-start.1) | collective-permute-done | bytes 1310752 | tf_op jit(solution)/shard_map/ppermute | solution.py:454
  17.3 28.3 %all_to_all.15 = f32[64,40,128]{2,1,0:T(8,128)} all-to-all(f32[64,40,128]{2,1,0:T(8,128)S(1)} %bitcast.28), channel_id=1, replica_groups=mesh['z'=4,'core'=2,'narrow'=16] {'z','narrow'}, dimensions={0} | all-to-all | bytes 2621440 | tf_op jit(solution)/shard_map/all_to_all | solution.py:456
  45.6 1.5 %reduce_sum.9 = f32[40,128]{1,0:T(8,128)S(1)} reduce(f32[64,40,128]{2,1,0:T(8,128)} %all_to_all.15, f32[]{:T(128)} %constant.32.clone.1), dimensions={0}, to_apply=%region_0.0 | reduce | flops 322560 | bytes 1331204 | tf_op jit(solution)/shard_map/reduce_sum | solution.py:459
  47.9 3.6 %all-to-all-start.1 = ((f32[16,40,128]{2,1,0:T(8,128)}), f32[16,40,128]{2,1,0:T(8,128)S(1)}, u32[]{:S(2)}, u32[]{:S(2)}) async-start(f32[16,40,128]{2,1,0:T(8,128)} %broadcast_in_dim.9), calls=%async_computation.1 | async-start | bytes 655360 | tf_op jit(solution)/shard_map/all_to_all | solution.py:460
  51.5 7.6 %all-to-all-done.1 = f32[16,40,128]{2,1,0:T(8,128)S(1)} async-done(((f32[16,40,128]{2,1,0:T(8,128)}), f32[16,40,128]{2,1,0:T(8,128)S(1)}, u32[]{:S(2)}, u32[]{:S(2)}) %all-to-all-start.1) | async-done | bytes 327712 | tf_op jit(solution)/shard_map/all_to_all | solution.py:460
  59.1 25.1 %solve_block.1 = bf16[256,128]{1,0:T(8,128)(2,1)S(1)} custom-call(f32[640,128]{1,0:T(8,128)S(1)} %bitcast.23, f32[1,256,256]{2,1,0:T(8,128)S(1)} %copy-done.9), custom_call_target="tpu_custom_call" | custom-call | tf_op jit(solution)/shard_map/solve_block/pallas_call | solution.py:193
  84.4 1.6 %collective-permute-start.3 = (bf16[256,128]{1,0:T(8,128)(2,1)S(1)}, bf16[256,128]{1,0:T(8,128)(2,1)S(1)}, u32[]{:S(2)}, u32[]{:S(2)}) collective-permute-start(bf16[256,128]{1,0:T(8,128)(2,1)S(1)} %solve_block.1), channel_id=1, source_target_pairs={{0,64},{32,96},{64,0},{96,32},{1,65},{33,97},{65,1},{97,33},{2,66}... | collective-permute-start | bytes 196616 | tf_op jit(solution)/shard_map/ppermute | solution.py:465
  86.0 1.3 collective-permute-start.4
  88.5 1.6 %copy-done.7 = bf16[4,512,512]{2,1,0:T(8,128)(2,1)S(1)} copy-done((bf16[4,512,512]{2,1,0:T(8,128)(2,1)S(1)}, bf16[4,512,512]{2,1,0:T(8,128)(2,1)}, u32[]{:S(2)}) %copy-start.7) | copy-done | bytes 2097176
  90.1 1.3 neumann_half.1.part
  91.4 4.6 %collective-permute-start.5 = (bf16[4,256,128]{2,1,0:T(8,128)(2,1)S(1)}, bf16[4,256,128]{2,1,0:T(8,128)(2,1)S(1)}, u32[]{:S(2)}, u32[]{:S(2)}) collective-permute-start(bf16[4,256,128]{2,1,0:T(8,128)(2,1)S(1)} %get-tuple-element.25), channel_id=1, source_target_pairs={{0,16},{16,0},{1,17},{17,1},{2,18},{18,2},{3,19},{19,3},{4,20},{20... | collective-permute-start | bytes 786440 | tf_op jit(solution)/shard_map/ppermute | solution.py:467
  96.1 4.0 %copy-done = bf16[4,1152,1152]{2,1,0:T(8,128)(2,1)S(1)} copy-done((bf16[4,1152,1152]{2,1,0:T(8,128)(2,1)S(1)}, bf16[4,1152,1152]{2,1,0:T(8,128)(2,1)}, u32[]{:S(2)}) %copy-start) | copy-done | bytes 10616856
  100.1 2.3 %copy-done.2 = bf16[4,512,1152]{2,1,0:T(8,128)(2,1)S(1)} copy-done((bf16[4,512,1152]{2,1,0:T(8,128)(2,1)S(1)}, bf16[4,512,1152]{2,1,0:T(8,128)(2,1)}, u32[]{:S(2)}) %copy-start.2) | copy-done | bytes 4718616
  102.4 8.8 %direction_action.1.moved = f32[4,512,128]{2,1,0:T(8,128)S(1)} custom-call(bf16[4,512,512]{2,1,0:T(8,128)(2,1)S(1)} %copy-done.4, bf16[4,512,1152]{2,1,0:T(8,128)(2,1)S(1)} %copy-done.2, bf16[4,1152,1152]{2,1,0:T(8,128)(2,1)S(1)} %copy-done, f32[4,256,128]{2,1,0:T(8,128)S(1)} %copy-done.5, f32[256,128]{1,0:T(8,128)S(1)} %collective-permute-done.8.halo.direction_halo), custom_call_target="tpu_custom_call" | custom-call | flops 2835349504 | bytes 17432576 | tf_op jit(solution)/shard_map/direction_action/pallas_call | solution.py:287
  111.3 1.5 %coarse_part.1.pre = f32[4,512,128]{2,1,0:T(8,128)S(1)} custom-call(s32[4]{0:T(128)S(1)} %fusion.1.own, bf16[4,512,256]{2,1,0:T(8,128)(2,1)S(1)} %get-tuple-element.12.spread, bf16[8,256,128]{2,1,0:T(8,128)(2,1)S(1)} %bitcast.22, f32[4,512,128]{2,1,0:T(8,128)S(1)} %neumann_half.1.part), custom_call_target="tpu_custom_call" | custom-call | tf_op jit(solution)/shard_map/coarse_part/pallas_call | solution.py:238
  113.4 4.3 %collective-permute-start.7 = (f32[256,128]{1,0:T(8,128)S(1)}, f32[256,128]{1,0:T(8,128)S(1)}, u32[]{:S(2)}, u32[]{:S(2)}) collective-permute-start(f32[256,128]{1,0:T(8,128)S(1)} %get-tuple-element.22), channel_id=1, source_target_pairs={{1,0},{2,1},{3,2},{4,3},{5,4},{6,5},{7,6},{8,7},{9,8},{10,9},{11,1... | collective-permute-start | bytes 393224 | tf_op jit(solution)/shard_map/ppermute | solution.py:476
  117.7 4.4 %search_action.2 = (f32[2,512,128]{2,1,0:T(8,128)S(1)}, f32[4,128]{1,0:T(4,128)S(1)}) custom-call(bf16[4,512,512]{2,1,0:T(8,128)(2,1)S(1)} %copy-done.4, bf16[4,512,1152]{2,1,0:T(8,128)(2,1)S(1)} %copy-done.3, bf16[4,1152,1152]{2,1,0:T(8,128)(2,1)S(1)} %copy-done.1, f32[4,512,128]{2,1,0:T(8,128)S(1)} %coarse_part.1.pre, f32[4,256,128]{2,1,0:T(8,128)S(1)} %copy-done.5, ...), custom_call_target="tpu_custom_call" | custom-call | flops 1417674752 | bytes 8716288 | tf_op jit(solution)/shard_map/search_action/pallas_call | solution.py:373
  122.2 4.5 %search_action.3 = (f32[2,512,128]{2,1,0:T(8,128)S(1)}, f32[4,128]{1,0:T(4,128)S(1)}) custom-call(bf16[4,512,512]{2,1,0:T(8,128)(2,1)S(1)} %copy-done.4, bf16[4,512,1152]{2,1,0:T(8,128)(2,1)S(1)} %copy-done.3, bf16[4,1152,1152]{2,1,0:T(8,128)(2,1)S(1)} %copy-done.1, f32[4,512,128]{2,1,0:T(8,128)S(1)} %coarse_part.1.pre, ...), custom_call_target="tpu_custom_call" | custom-call | flops 1417674752 | bytes 8716288 | tf_op jit(solution)/shard_map/search_action/pallas_call | solution.py:373
  126.9 19.9 %all_to_all.16.sums = f32[128,4,128]{2,1,0:T(4,128)S(1)} all-to-all(f32[128,4,128]{2,1,0:T(4,128)S(1)} %broadcast_in_dim.20), channel_id=1, replica_groups=mesh['z'=4,'core'=2,'narrow'=16] {'z','core','narrow'}, dimensions={0} | all-to-all | bytes 524288 | tf_op jit(solution)/shard_map/all_to_all | solution.py:498
  146.8 1.3 update.1
  (54 shorter events, 5.1 us)
Async XLA Ops:
  0.6 8.3 %copy-start.6 = (f32[4,256,128]{2,1,0:T(8,128)S(1)}, f32[4,256,128]{2,1,0:T(8,128)}, u32[]{:S(2)}) copy-start(f32[4,256,128]{2,1,0:T(8,128)} %residual.5) | copy-start | bytes 1572868
  0.6 8.2 %copy-start.14 = (s32[4,200]{1,0:T(4,128)S(1)}, s32[4,200]{1,0:T(4,128)}, u32[]{:S(2)}) copy-start(s32[4,200]{1,0:T(4,128)} %param.26) | copy-start | bytes 9604
  0.7 8.3 %copy-start.10 = (s32[4,1]{0,1:T(1,128)S(1)}, s32[4,1]{0,1:T(1,128)}, u32[]{:S(2)}) copy-start(s32[4,1]{0,1:T(1,128)} %param.25) | copy-start | bytes 52
  0.7 8.3 %copy-start.12 = (bf16[4,200,200]{2,1,0:T(8,128)(2,1)S(1)}, bf16[4,200,200]{2,1,0:T(8,128)(2,1)}, u32[]{:S(2)}) copy-start(bf16[4,200,200]{2,1,0:T(8,128)(2,1)} %panel.1) | copy-start | bytes 960004
  0.7 8.3 %copy-start.13 = (s32[4]{0:T(128)S(1)}, s32[4]{0:T(128)}, u32[]{:S(2)}) copy-start(s32[4]{0:T(128)} %chg.1) | copy-start | bytes 52
  1.7 10.6 %collective-permute-start = (bf16[256,128]{1,0:T(8,128)(2,1)S(1)}, bf16[256,128]{1,0:T(8,128)(2,1)S(1)}, u32[]{:S(2)}, u32[]{:S(2)}) collective-permute-start(bf16[256,128]{1,0:T(8,128)(2,1)S(1)} %fusion), channel_id=1, source_target_pairs={{1,0},{2,1},{3,2},{4,3},{5,4},{6,5},{7,6},{8,7},{9,8},{10,9},{11,1... | collective-permute-start | bytes 196616 | tf_op jit(solution)/shard_map/ppermute | solution.py:447
  13.4 3.7 %collective-permute-start.1 = (f32[4,640,128]{2,1,0:T(8,128)S(1)}, f32[4,640,128]{2,1,0:T(8,128)S(1)}, u32[]{:S(2)}, u32[]{:S(2)}) collective-permute-start(f32[4,640,128]{2,1,0:T(8,128)S(1)} %get-tuple-element.16), channel_id=1, source_target_pairs={{0,16},{16,0},{1,17},{17,1},{2,18},{18,2},{3,19},{19,3},{4,20},{20... | collective-permute-start | bytes 3932168 | tf_op jit(solution)/shard_map/ppermute | solution.py:454
  45.6 5.8 %copy-start.5 = (f32[4,256,128]{2,1,0:T(8,128)S(1)}, f32[4,256,128]{2,1,0:T(8,128)}, u32[]{:S(2)}) copy-start(f32[4,256,128]{2,1,0:T(8,128)} %direction.7) | copy-start | bytes 1572868
  45.6 13.5 %copy-start.9 = (f32[1,256,256]{2,1,0:T(8,128)S(1)}, f32[1,256,256]{2,1,0:T(8,128)}, u32[]{:S(2)}) copy-start(f32[1,256,256]{2,1,0:T(8,128)} %base.1) | copy-start | bytes 786436
  47.9 11.2 %all-to-all-start.1 = ((f32[16,40,128]{2,1,0:T(8,128)}), f32[16,40,128]{2,1,0:T(8,128)S(1)}, u32[]{:S(2)}, u32[]{:S(2)}) async-start(f32[16,40,128]{2,1,0:T(8,128)} %broadcast_in_dim.9), calls=%async_computation.1 | async-start | bytes 655360 | tf_op jit(solution)/shard_map/all_to_all | solution.py:460
  84.3 7.1 %collective-permute-start.2 = (bf16[256,128]{1,0:T(8,128)(2,1)S(1)}, bf16[256,128]{1,0:T(8,128)(2,1)S(1)}, u32[]{:S(2)}, u32[]{:S(2)}) collective-permute-start(bf16[256,128]{1,0:T(8,128)(2,1)S(1)} %solve_block.1), channel_id=1, source_target_pairs={{0,32},{32,64},{64,96},{96,0},{1,33},{33,65},{65,97},{97,1},{2,34}... | collective-permute-start | bytes 196616 | tf_op jit(solution)/shard_map/ppermute | solution.py:465
  84.4 6.9 %collective-permute-start.3 = (bf16[256,128]{1,0:T(8,128)(2,1)S(1)}, bf16[256,128]{1,0:T(8,128)(2,1)S(1)}, u32[]{:S(2)}, u32[]{:S(2)}) collective-permute-start(bf16[256,128]{1,0:T(8,128)(2,1)S(1)} %solve_block.1), channel_id=1, source_target_pairs={{0,64},{32,96},{64,0},{96,32},{1,65},{33,97},{65,1},{97,33},{2,66}... | collective-permute-start | bytes 196616 | tf_op jit(solution)/shard_map/ppermute | solution.py:465
  86.0 5.3 %collective-permute-start.4 = (bf16[256,128]{1,0:T(8,128)(2,1)S(1)}, bf16[256,128]{1,0:T(8,128)(2,1)S(1)}, u32[]{:S(2)}, u32[]{:S(2)}) collective-permute-start(bf16[256,128]{1,0:T(8,128)(2,1)S(1)} %solve_block.1), channel_id=1, source_target_pairs={{0,96},{32,0},{64,32},{96,64},{1,97},{33,1},{65,33},{97,65},{2,98}... | collective-permute-start | bytes 196616 | tf_op jit(solution)/shard_map/ppermute | solution.py:465
  87.4 8.7 %collective-permute-start.8 = (f32[256,128]{1,0:T(8,128)S(1)}, f32[256,128]{1,0:T(8,128)S(1)}, u32[]{:S(2)}, u32[]{:S(2)}) collective-permute-start(f32[256,128]{1,0:T(8,128)S(1)} %slice_bitcast_fusion.2), channel_id=1, source_target_pairs={{1,0},{2,1},{3,2},{4,3},{5,4},{6,5},{7,6},{8,7},{9,8},{10,9},{11,1... | collective-permute-start | bytes 393224 | tf_op jit(solution)/shard_map/ppermute | solution.py:453
  90.1 6.0 %copy-start.4 = (bf16[4,512,512]{2,1,0:T(8,128)(2,1)S(1)}, bf16[4,512,512]{2,1,0:T(8,128)(2,1)}, u32[]{:S(2)}) copy-start(bf16[4,512,512]{2,1,0:T(8,128)(2,1)} %stiffness.5) | copy-start | bytes 6291460
  91.4 19.8 %collective-permute-start.5 = (bf16[4,256,128]{2,1,0:T(8,128)(2,1)S(1)}, bf16[4,256,128]{2,1,0:T(8,128)(2,1)S(1)}, u32[]{:S(2)}, u32[]{:S(2)}) collective-permute-start(bf16[4,256,128]{2,1,0:T(8,128)(2,1)S(1)} %get-tuple-element.25), channel_id=1, source_target_pairs={{0,16},{16,0},{1,17},{17,1},{2,18},{18,2},{3,19},{19,3},{4,20},{20... | collective-permute-start | bytes 786440 | tf_op jit(solution)/shard_map/ppermute | solution.py:467
  96.1 4.0 %copy-start = (bf16[4,1152,1152]{2,1,0:T(8,128)(2,1)S(1)}, bf16[4,1152,1152]{2,1,0:T(8,128)(2,1)}, u32[]{:S(2)}) copy-start(bf16[4,1152,1152]{2,1,0:T(8,128)(2,1)} %interior.5) | copy-start | bytes 31850500
  102.4 15.3 %copy-start.1 = (bf16[4,1152,1152]{2,1,0:T(8,128)(2,1)S(1)}, bf16[4,1152,1152]{2,1,0:T(8,128)(2,1)}, u32[]{:S(2)}) copy-start(bf16[4,1152,1152]{2,1,0:T(8,128)(2,1)} %interior.5) | copy-start | bytes 31850500
  111.2 6.5 %copy-start.3 = (bf16[4,512,1152]{2,1,0:T(8,128)(2,1)S(1)}, bf16[4,512,1152]{2,1,0:T(8,128)(2,1)}, u32[]{:S(2)}) copy-start(bf16[4,512,1152]{2,1,0:T(8,128)(2,1)} %coupling.5) | copy-start | bytes 14155780
  112.8 9.3 %collective-permute-start.6 = (f32[256,128]{1,0:T(8,128)S(1)}, f32[256,128]{1,0:T(8,128)S(1)}, u32[]{:S(2)}, u32[]{:S(2)}) collective-permute-start(f32[256,128]{1,0:T(8,128)S(1)} %get-tuple-element.23), channel_id=1, source_target_pairs={{0,1},{1,2},{2,3},{3,4},{4,5},{5,6},{6,7},{7,8},{8,9},{9,10},{10,1... | collective-permute-start | bytes 393224 | tf_op jit(solution)/shard_map/ppermute | solution.py:475
  113.4 8.8 %collective-permute-start.7 = (f32[256,128]{1,0:T(8,128)S(1)}, f32[256,128]{1,0:T(8,128)S(1)}, u32[]{:S(2)}, u32[]{:S(2)}) collective-permute-start(f32[256,128]{1,0:T(8,128)S(1)} %get-tuple-element.22), channel_id=1, source_target_pairs={{1,0},{2,1},{3,2},{4,3},{5,4},{6,5},{7,6},{8,7},{9,8},{10,9},{11,1... | collective-permute-start | bytes 393224 | tf_op jit(solution)/shard_map/ppermute | solution.py:476
  126.7 20.1 %copy-start.8 = (f32[4,256,128]{2,1,0:T(8,128)S(1)}, f32[4,256,128]{2,1,0:T(8,128)}, u32[]{:S(2)}) copy-start(f32[4,256,128]{2,1,0:T(8,128)} %solution.1) | copy-start | bytes 1572868
  126.7 20.1 %copy-start.11 = (f32[128]{0:T(128)S(1)}, f32[128]{0:T(128)}, u32[]{:S(2)}) copy-start(f32[128]{0:T(128)} %param.17) | copy-start | bytes 1540
  126.7 20.0 %collective-permute-start.9 = (f32[2,256,128]{2,1,0:T(8,128)S(1)}, f32[2,256,128]{2,1,0:T(8,128)S(1)}, u32[]{:S(2)}, u32[]{:S(2)}) collective-permute-start(f32[2,256,128]{2,1,0:T(8,128)S(1)} %pad_maximum_fusion.2), channel_id=1, source_target_pairs={{0,1},{1,2},{2,3},{3,4},{4,5},{5,6},{6,7},{7,8},{8,9},{9,10},{10,1... | collective-permute-start | bytes 786440 | tf_op jit(solution)/shard_map/ppermute | solution.py:497
  (2 other events, 3.9 us)

commit v2 on v1

v2 whole, which is shorter than its diff:
```python
import jax
import jax.numpy as jnp
from jax import lax
from jax.experimental import pallas as pl
from jax.experimental.pallas import tpu as pltpu
from jax.sharding import Mesh, PartitionSpec as P

F32 = jnp.float32
BF16 = jnp.bfloat16
NN = (((1,), (0,)), ((), ()))
NT = (((1,), (1,)), ((), ()))
TN = (((0,), (0,)), ((), ()))
SMALL = 16 * 1024 * 1024
LARGE = 24 * 1024 * 1024
HIGHEST = lax.Precision.HIGHEST


def dot(a, b, dims=NN, precision=None):
    return lax.dot_general(a, b, dims, precision=precision, preferred_element_type=F32)


def smem():
    return pl.BlockSpec(memory_space=pltpu.SMEM)


def whole(shape):
    return pl.BlockSpec(shape, lambda *_: (0,) * len(shape))


def params(limit=SMALL):
    return pltpu.CompilerParams(vmem_limit_bytes=limit)


def column_sum(value):
    return jnp.sum(value, axis=0, keepdims=True)


def place_kernel(own, chg, core, pm, basis, panel, res, keep, send, spread):
    s = pl.program_id(0)
    co = spread.shape[1]
    half = co // 2
    face = res.shape[1]

    @pl.when(s == 0)
    def _():
        keep[...] = jnp.zeros_like(keep)
        send[...] = jnp.zeros_like(send)

    rows = lax.broadcasted_iota(jnp.int32, (co, pm.shape[2]), 0)
    select = (rows == pm[0]).astype(F32).astype(BF16)
    wide_basis = dot(select, basis[0]).astype(BF16)
    spread[0] = wide_basis
    placed = dot(dot(select, panel[0]).astype(BF16), select, NT) * chg[s].astype(F32)
    last = pl.num_programs(0) - 1
    here = res[s].astype(BF16)
    there = res[jnp.minimum(s + 1, last)].astype(BF16)
    rhs = dot(wide_basis[:, :face], here)
    rhs += jnp.where(s < last, dot(wide_basis[:, face:], there), 0.0)
    owner = own[s]
    place = owner >> 1
    other = (owner & 1) != core[0]

    def add(to):
        to[place, 0:half] += placed[:half, :half]
        to[place, half:co] += placed[half:, :half]
        to[place, co : co + half] += placed[half:, half:]
        to[place, co + half :] += rhs

    @pl.when(other)
    def _():
        add(send)

    @pl.when(jnp.logical_not(other))
    def _():
        add(keep)


def place_panels(own, chg, core, prim_map, basis, panels, residual, groups):
    subs, npr, nb = basis.shape
    co = 2 * residual.shape[2]
    rows = 3 * (co // 2) + co
    packed = (groups, rows, co // 2)
    return pl.pallas_call(
        place_kernel,
        grid=(subs,),
        in_specs=[
            smem(),
            smem(),
            smem(),
            pl.BlockSpec((1, 1, npr), lambda s: (s, 0, 0)),
            pl.BlockSpec((1, npr, nb), lambda s: (s, 0, 0)),
            pl.BlockSpec((1, npr, npr), lambda s: (s, 0, 0)),
            whole(residual.shape),
        ],
        out_specs=[whole(packed), whole(packed), pl.BlockSpec((1, co, nb), lambda s: (s, 0, 0))],
        out_shape=[
            jax.ShapeDtypeStruct(packed, F32),
            jax.ShapeDtypeStruct(packed, F32),
            jax.ShapeDtypeStruct((subs, co, nb), BF16),
        ],
        compiler_params=params(),
        cost_estimate=pl.CostEstimate(flops=10**9, bytes_accessed=6 * 10**6, transcendentals=0),
        name="place_panels",
    )(own, chg, core, prim_map, basis, panels, residual)


def halo_kernel(own, core, spread, halo, keep_in, send_in, keep, send, held, sem):
    del keep_in, send_in
    owner = own[own.shape[0] - 1]
    place = owner >> 1
    other = (owner & 1) != core[0]
    rows = held.shape[0]

    def add(to):
        part = to.at[place, pl.ds(to.shape[1] - rows, rows)]
        fetch = pltpu.make_async_copy(part, held, sem)
        fetch.start()
        value = dot(spread[0], halo[...])
        fetch.wait()
        held[...] += value
        put = pltpu.make_async_copy(held, part, sem)
        put.start()
        put.wait()

    @pl.when(other)
    def _():
        add(send)

    @pl.when(jnp.logical_not(other))
    def _():
        add(keep)


def add_halo(own, core, spread, halo, keep, send):
    subs, co, nb = spread.shape
    hbm = pl.BlockSpec(memory_space=pl.ANY)
    return pl.pallas_call(
        halo_kernel,
        grid=(1,),
        in_specs=[
            smem(),
            smem(),
            pl.BlockSpec((1, co, nb // 2), lambda _: (subs - 1, 0, 1)),
            whole(halo.shape),
            hbm,
            hbm,
        ],
        out_specs=[hbm, hbm],
        out_shape=[jax.ShapeDtypeStruct(keep.shape, F32), jax.ShapeDtypeStruct(send.shape, F32)],
        input_output_aliases={4: 0, 5: 1},
        scratch_shapes=[pltpu.VMEM((co, halo.shape[1]), F32), pltpu.SemaphoreType.DMA],
        compiler_params=params(),
        name="add_halo",
    )(own, core, spread, halo, keep, send)


def gather_kernel(parts, out):
    total = jnp.sum(parts[...], axis=0)
    for i in range(out.shape[0]):
        out[i] = total


def sum_copies(parts, copies):
    return pl.pallas_call(
        gather_kernel,
        out_shape=jax.ShapeDtypeStruct((copies,) + parts.shape[1:], F32),
        compiler_params=params(),
        name="sum_copies",
    )(parts)


MOST_STEPS = 24


def inverse(matrix):
    n = matrix.shape[0]
    lanes = lax.broadcasted_iota(jnp.int32, (8, n), 1)
    subl = lax.broadcasted_iota(jnp.int32, (8, n), 0)
    tiles = tuple(matrix[8 * i : 8 * i + 8] for i in range(n // 8))

    def group(_, tiles):
        tiles = list(tiles)
        for j in range(8):
            pivot_row = tiles[0][j : j + 1, :]
            scale = 1.0 / pivot_row[:, j : j + 1]
            row = jnp.where(lanes[:1] == j, scale, pivot_row * scale)
            for i, tile in enumerate(tiles):
                new = jnp.where(lanes == j, 0.0, tile) - tile[:, j : j + 1] * row
                if i == 0:
                    new = jnp.where(subl == j, row, new)
                tiles[i] = new
        return tuple(pltpu.roll(tile, n - 8, 1) for tile in tiles[1:] + tiles[:1])

    return jnp.concatenate(lax.fori_loop(0, n // 8, group, tiles), axis=0)


def split(value, terms):
    found = []
    for _ in range(terms):
        found.append(value.astype(BF16))
        value = value - found[-1].astype(F32)
    return found


def eliminate(matrix, right):
    half = matrix.shape[0] // 2
    a21 = matrix[half:, :half]
    b1, b2 = right[:half], right[half:]
    inv1 = inverse(matrix[:half, :half])
    carry = dot(a21, inv1, NN, HIGHEST)
    inv2 = inverse(matrix[half:, half:] - dot(carry, a21, NT, HIGHEST))
    x2 = dot(inv2, b2 - dot(carry, b1, NN, HIGHEST), NN, HIGHEST)
    x1 = dot(inv1, b1, NN, HIGHEST) - dot(carry, x2, TN, HIGHEST)
    return x1, x2


def solve_kernel(packed, base, out, mat, terms, x, r, p):
    co = out.shape[0]
    half = co // 2
    a21 = packed[half:co]
    mat[:half, :half] = packed[:half] + base[0, :half, :half]
    mat[half:, :half] = a21 + base[0, half:, :half]
    mat[:half, half:] = a21.T + base[0, :half, half:]
    mat[half:, half:] = packed[co : co + half] + base[0, half:, half:]
    rows = lax.broadcasted_iota(jnp.int32, (co, co), 0)
    columns = lax.broadcasted_iota(jnp.int32, (co, co), 1)
    scale = 1.0 / jnp.sum(jnp.where(rows == columns, mat[...], 0.0), axis=1, keepdims=True)
    for i, term in enumerate(split(mat[...], 3)):
        terms[i] = term
    right = packed[co + half :]
    size = jnp.max(jnp.abs(right), axis=0, keepdims=True)
    size = jnp.where(size > 0.0, size, 1.0)
    right = right * (1.0 / size)

    def times(value):
        n = value.shape[1]
        v1, v2, v3 = split(value, 3)
        pair = jnp.concatenate([v1, v2], axis=1)
        first = dot(terms[0], pair)
        second = dot(terms[1], pair)
        small = second[:, n:] + dot(terms[0], v3) + dot(terms[2], v1)
        return first[:, :n] + (first[:, n:] + second[:, :n] + small)

    x[...] = jnp.zeros_like(right)
    r[...] = right
    p[...] = scale * right
    start = column_sum(right * (scale * right))

    def steps(state):
        count, norm, _ = state
        for _ in range(2):
            image = times(p[...])
            energy = column_sum(p[...] * image)
            length = jnp.where(energy > 0.0, norm / energy, 0.0)
            x[...] += length * p[...]
            left = r[...] - length * image
            r[...] = left
            scaled = scale * left
            new = column_sum(left * scaled)
            p[...] = scaled + jnp.where(norm > 0.0, new / norm, 0.0) * p[...]
            norm = new
        return count + 2, norm, jnp.max(norm - 1e-13 * start) > 0.0

    lax.while_loop(
        lambda state: state[2] & (state[0] < MOST_STEPS), steps, (jnp.int32(0), start, jnp.bool_(True))
    )
    left = right - dot(mat[...], x[...], NN, HIGHEST)
    solved = jnp.max(column_sum(left * (scale * left)) - 1e-11 * start) <= 0.0

    @pl.when(solved)
    def _():
        out[...] = (x[...] * size).astype(BF16)

    @pl.when(jnp.logical_not(solved))
    def _():
        x1, x2 = eliminate(mat[...], packed[co + half :])
        out[:half] = x1.astype(BF16)
        out[half:] = x2.astype(BF16)


def solve_block(packed, base):
    co = base.shape[1]
    rhs = packed.shape[1]
    return pl.pallas_call(
        solve_kernel,
        out_shape=jax.ShapeDtypeStruct((co, rhs), BF16),
        scratch_shapes=[
            pltpu.VMEM((co, co), F32),
            pltpu.VMEM((3, co, co), BF16),
            pltpu.VMEM((co, rhs), F32),
            pltpu.VMEM((co, rhs), F32),
            pltpu.VMEM((co, rhs), F32),
        ],
        compiler_params=params(),
        name="solve_block",
    )(packed, base)


def neumann_kernel(neumann, spread, res, halo, out, turned):
    s = pl.program_id(0)
    last = pl.num_programs(0) - 1
    here = res[s].astype(BF16)
    there = jnp.where(s < last, res[jnp.minimum(s + 1, last)], halo[...].astype(F32)).astype(BF16)
    out[0] = 0.5 * dot(neumann[0], jnp.concatenate([here, there], axis=0))
    turned[0] = spread[0].T


def neumann_half(neumann, spread, residual, halo):
    subs, co, nb = spread.shape
    rhs = residual.shape[2]
    return pl.pallas_call(
        neumann_kernel,
        grid=(subs,),
        in_specs=[
            pl.BlockSpec((1, nb, nb), lambda s: (s, 0, 0)),
            pl.BlockSpec((1, co, nb), lambda s: (s, 0, 0)),
            whole(residual.shape),
            whole(halo.shape),
        ],
        out_specs=[
            pl.BlockSpec((1, nb, rhs), lambda s: (s, 0, 0)),
            pl.BlockSpec((1, nb, co), lambda s: (s, 0, 0)),
        ],
        out_shape=[
            jax.ShapeDtypeStruct((subs, nb, rhs), F32),
            jax.ShapeDtypeStruct((subs, nb, co), BF16),
        ],
        compiler_params=params(),
        cost_estimate=pl.CostEstimate(
            flops=2 * subs * nb * nb * rhs, bytes_accessed=4 * 10**6, transcendentals=0
        ),
        name="neumann_half",
    )(neumann, spread, residual, halo)


def coarse_kernel(other, turn, turned, ring, twin, part, out, near, far):
    s = pl.program_id(0)
    face = near.shape[0]
    at = turn[s]
    solved = jnp.where(other[s] == 1, twin[at].astype(F32), ring[at].astype(F32)).astype(BF16)
    found = part[0] + 0.5 * dot(turned[0], solved)
    out[0] = found

    @pl.when(s == 0)
    def _():
        near[...] = found[:face]

    @pl.when(s == pl.num_programs(0) - 1)
    def _():
        far[...] = found[face:]


def coarse_part(other, turn, turned, ring, twin, part):
    subs, nb, co = turned.shape
    rhs = ring.shape[2]
    return pl.pallas_call(
        coarse_kernel,
        grid=(subs,),
        in_specs=[
            smem(),
            smem(),
            pl.BlockSpec((1, nb, co), lambda s: (s, 0, 0)),
            whole(ring.shape),
            whole(twin.shape),
            pl.BlockSpec((1, nb, rhs), lambda s: (s, 0, 0)),
        ],
        out_specs=[
            pl.BlockSpec((1, nb, rhs), lambda s: (s, 0, 0)),
            whole((nb // 2, rhs)),
            whole((nb // 2, rhs)),
        ],
        out_shape=[
            jax.ShapeDtypeStruct((subs, nb, rhs), F32),
            jax.ShapeDtypeStruct((nb // 2, rhs), F32),
            jax.ShapeDtypeStruct((nb // 2, rhs), F32),
        ],
        compiler_params=params(),
        name="coarse_part",
    )(other, turn, turned, ring, twin, part)


def action(stiffness, coupling, interior, field):
    load = dot(coupling, field, TN).astype(BF16)
    inside = dot(interior, load).astype(BF16)
    return dot(stiffness, field) - dot(coupling, inside)


def operators(nb, ni, place):
    return [
        pl.BlockSpec((1, nb, nb), place),
        pl.BlockSpec((1, nb, ni), place),
        pl.BlockSpec((1, ni, ni), place),
    ]


def cost(steps, nb, ni, rhs):
    return pl.CostEstimate(
        flops=2 * steps * rhs * (nb * nb + 2 * nb * ni + ni * ni),
        bytes_accessed=2 * steps * (nb * nb + nb * ni + ni * ni),
        transcendentals=0,
    )


def act(stiffness, coupling, interior, own_p, far_p, own_d, far_d, own_r):
    face, rhs = own_p.shape
    field = jnp.concatenate(
        [jnp.concatenate([own_p, own_d], axis=1), jnp.concatenate([far_p, far_d], axis=1)], axis=0
    )
    both = action(stiffness[0], coupling[0], interior[0], field.astype(BF16))
    image, moved = both[:, :rhs], both[:, rhs:]
    parts = jnp.concatenate(
        [
            column_sum(own_r * own_p),
            column_sum(own_p * image[:face] + far_p * image[face:]),
            column_sum(own_p * moved[:face] + far_p * moved[face:])
            + column_sum(own_d * image[:face] + far_d * image[face:]),
            column_sum(own_d * moved[:face] + far_d * moved[face:]),
        ],
        axis=0,
    )
    return both, parts


def inner_kernel(stiffness, coupling, interior, pre, direction, residual, out, sums):
    i = pl.program_id(0)
    s = i + 1
    face = direction.shape[1]
    own_p = pre[s, :face] + pre[s - 1, face:]
    far_p = pre[s + 1, :face] + pre[s, face:]
    out[0], parts = act(
        stiffness, coupling, interior, own_p, far_p, direction[s], direction[s + 1], residual[s]
    )

    @pl.when(i == 0)
    def _():
        sums[...] = parts

    @pl.when(i > 0)
    def _():
        sums[...] += parts


def outer_kernel(
    stiffness,
    coupling,
    interior,
    pre,
    from_prev,
    from_next,
    direction,
    direction_halo,
    residual,
    earlier,
    out,
    copies,
    far,
    sums,
):
    i = pl.program_id(0)
    last = direction.shape[0] - 1
    s = i * last
    near = jnp.minimum(s + 1, last)
    behind = jnp.maximum(s - 1, 0)
    face = direction.shape[1]
    own_p = pre[s, :face] + jnp.where(i == 0, from_prev[...], pre[behind, face:])
    far_p = pre[s, face:] + jnp.where(i == 0, pre[near, :face], from_next[...])
    far_d = jnp.where(i == 0, direction[near], direction_halo[...])
    both, parts = act(
        stiffness, coupling, interior, own_p, far_p, direction[s], far_d, residual[s]
    )
    out[0] = both

    @pl.when(i == 0)
    def _():
        sums[...] = earlier[...] + parts

    @pl.when(i > 0)
    def _():
        far[...] = both[face:]
        total = sums[...] + parts
        for k in range(copies.shape[0]):
            copies[k] = total


def search_inner(stiffness, coupling, interior, pre, direction, residual):
    subs, nb, ni = coupling.shape
    rhs = direction.shape[2]
    rest = (pre, direction, residual)
    return pl.pallas_call(
        inner_kernel,
        grid=(subs - 2,),
        in_specs=operators(nb, ni, lambda i: (i + 1, 0, 0)) + [whole(x.shape) for x in rest],
        out_specs=[pl.BlockSpec((1, nb, 2 * rhs), lambda i: (i, 0, 0)), whole((4, rhs))],
        out_shape=[
            jax.ShapeDtypeStruct((subs - 2, nb, 2 * rhs), F32),
            jax.ShapeDtypeStruct((4, rhs), F32),
        ],
        compiler_params=params(LARGE),
        cost_estimate=cost(subs - 2, nb, ni, 2 * rhs),
        name="search_inner",
    )(stiffness, coupling, interior, *rest)


def search_outer(devices, stiffness, coupling, interior, *rest):
    subs, nb, ni = coupling.shape
    rhs = rest[0].shape[2]
    return pl.pallas_call(
        outer_kernel,
        grid=(2,),
        in_specs=operators(nb, ni, lambda i: ((subs - 1) * i, 0, 0)) + [whole(x.shape) for x in rest],
        out_specs=[
            pl.BlockSpec((1, nb, 2 * rhs), lambda i: (i, 0, 0)),
            whole((devices, 4, rhs)),
            whole((nb // 2, 2 * rhs)),
        ],
        out_shape=[
            jax.ShapeDtypeStruct((2, nb, 2 * rhs), F32),
            jax.ShapeDtypeStruct((devices, 4, rhs), F32),
            jax.ShapeDtypeStruct((nb // 2, 2 * rhs), F32),
        ],
        scratch_shapes=[pltpu.VMEM((4, rhs), F32)],
        compiler_params=params(LARGE),
        cost_estimate=cost(2, nb, ni, 2 * rhs),
        name="search_outer",
    )(stiffness, coupling, interior, *rest)


def update_kernel(
    sums, last_inner, pre, from_prev, outer, inside, before, direction, residual, solution, new_sol, new_res
):
    total = jnp.sum(sums[...], axis=0)
    inner = total[0:1]
    beta = inner / last_inner[...]
    curvature = total[1:2] + beta * (total[2:3] + beta * total[3:4])
    step = inner / curvature
    subs, face, rhs = direction.shape
    last = subs - 1

    def part(s):
        return outer[0] if s == 0 else outer[1] if s == last else inside[s - 1]

    for s in range(subs):
        behind = from_prev[...] if s == 0 else pre[s - 1, face:]
        both = part(s)[:face] + (before[...] if s == 0 else part(s - 1)[face:])
        search = pre[s, :face] + behind + beta * direction[s]
        image = both[:, :rhs] + beta * both[:, rhs:]
        new_sol[s] = solution[s] + step * search
        new_res[s] = residual[s] - step * image


def update(*args):
    shape = jax.ShapeDtypeStruct(args[-1].shape, F32)
    return pl.pallas_call(
        update_kernel, out_shape=[shape, shape], compiler_params=params(), name="update"
    )(*args)


def local(
    solution,
    residual,
    direction,
    last_inner,
    stiffness,
    coupling,
    interior,
    neumann,
    basis,
    panels,
    base_coarse,
    owners,
    prim_map,
    changed,
):
    groups = lax.axis_size("z")
    pieces = lax.axis_size("narrow")
    devices = groups * 2 * pieces
    face, rhs = residual.shape[1:]
    forward = [(i, (i + 1) % pieces) for i in range(pieces)]
    back = [((i + 1) % pieces, i) for i in range(pieces)]
    own = owners[:, 0]
    core = lax.axis_index("core")
    core_ref = core.astype(jnp.int32).reshape(1)

    halo = lax.ppermute(residual[0].astype(BF16), "narrow", back)
    direction_halo = lax.ppermute(direction[0], "narrow", back)
    other = ((own & 1) != core).astype(jnp.int32)
    turn = ((lax.axis_index("z") - (own >> 1)) % groups).astype(jnp.int32)
    keep, send, spread = place_panels(
        own, changed, core_ref, prim_map[:, None, :], jnp.swapaxes(basis, 1, 2), panels, residual, groups
    )
    keep, send = add_halo(own, core_ref, spread, halo, keep, send)
    mine = keep + lax.ppermute(send, "core", [(0, 1), (1, 0)])
    rows = mine.shape[1] // pieces
    mine, direction_halo, other, turn = lax.optimization_barrier((mine, direction_halo, other, turn))
    parts = lax.all_to_all(
        mine.reshape(groups * pieces, rows, rhs), ("z", "narrow"), 0, 0, tiled=True
    )
    copies = sum_copies(parts, pieces)
    packed = lax.all_to_all(copies, "narrow", 0, 0, tiled=True)
    solved = solve_block(packed.reshape(pieces * rows, rhs), base_coarse)

    turns = [lax.ppermute(solved, "z", [(i, (i + d) % groups) for i in range(groups)]) for d in range(1, groups)]
    ring = jnp.stack([solved] + turns)
    twin = lax.ppermute(ring, "core", [(0, 1), (1, 0)])
    given, spread, _ = lax.optimization_barrier((residual, spread, solved))
    part, turned = neumann_half(neumann, spread, given, halo)
    pre, near, far = coarse_part(other, turn, turned, ring, twin, part)
    from_prev = lax.ppermute(far, "narrow", forward)
    from_next = lax.ppermute(near, "narrow", back)
    inside, sums = search_inner(stiffness, coupling, interior, pre, direction, residual)
    outer, sums, behind = search_outer(
        devices,
        stiffness,
        coupling,
        interior,
        pre,
        from_prev,
        from_next,
        direction,
        direction_halo,
        residual,
        sums,
    )
    before = lax.ppermute(behind, "narrow", forward)
    sums = lax.all_to_all(sums, ("z", "core", "narrow"), 0, 0, tiled=True)
    return tuple(
        update(
            sums,
            last_inner[None],
            pre,
            from_prev,
            outer,
            inside,
            before,
            direction,
            residual,
            solution,
        )
    )


def solution(mesh):
    wide, narrow = mesh.devices.shape
    finer = Mesh(mesh.devices.reshape(wide // 2, 2, narrow), ("z", "core", "narrow"))
    split = ("z", "core", "narrow")
    in_specs = (
        P(split, None, None),
        P(split, None, None),
        P(split, None, None),
        P(),
        P(split, None, None),
        P(split, None, None),
        P(split, None, None),
        P(split, None, None),
        P(split, None, None),
        P(split, None, None),
        P(("z", "core"), None, None),
        P(split, None),
        P(split, None),
        P(split),
    )
    out_specs = (P(split, None, None), P(split, None, None))
    return jax.shard_map(local, mesh=finer, in_specs=in_specs, out_specs=out_specs, check_vma=False)
```

time: 149 us -> 127 us (0.85)
  Pallas kernels: 51.3 us -> 24.8 us
  blocking collectives: 48.2 us -> 61.3 us
  waiting for transfers between devices: 10.3 us -> 5.2 us
  starting transfers between devices: 24.1 us -> 21 us
    pallas_call x5, Pallas kernels: 44.3 us -> 17.1 us  [the longest x1 5.66 us: search_outer(): pl.pallas_call(outer_kernel, grid=(2,), in_specs=operators(nb, ni, lambda...]
    all_to_all x1 -> x2, blocking collectives: 19.9 us -> 31 us  [the longest x1 19.7 us: local(): sums = lax.all_to_all(sums, ('z', 'core', 'narrow'), 0, 0, tiled=True)]
    all_to_all x1 -> x0, waiting for transfers between devices: 7.64 us -> none  [local(): lax.all_to_all(jnp.broadcast_to(piece[None], (pieces,) + piece.shape), 'n...]
    ppermute x3, waiting for transfers between devices: 0.01 us -> 3.58 us  [local(): lax.ppermute(solved, 'z', [(i, (i + d) % groups) for i in range(groups)])]
    all_to_all x1 -> x0, starting transfers between devices: 3.57 us -> none  [local(): lax.all_to_all(jnp.broadcast_to(piece[None], (pieces,) + piece.shape), 'n...]
    all_to_all x1, blocking collectives: 28.3 us -> 30.3 us  [local(): lax.all_to_all(mine.reshape(groups * pieces, rows, rhs), ('z', 'narrow'),...]
    add x1, other arithmetic: 0.2 us -> 1.99 us  [local(): mine = keep + lax.ppermute(send, 'core', [(0, 1), (1, 0)])]
    reduce_sum x1 -> x0, other arithmetic: 1.5 us -> none  [local(): piece = jnp.sum(parts, axis=0)]
  transfers between devices with their start and end apart: 11 -> 10, of which waited for: 2 -> 5; matrix products, arithmetic and copies ran while one was open for 1% -> 2% of each run, Pallas kernels for 12% -> 9%
where the time goes in v2:
time: 127 us; the launch traced here: 126 us
  blocking collectives  61.3 us (48%)
  Pallas kernels  24.8 us (20%)
  starting transfers between devices  21 us (17%)
  local copies, waits for them, and re-layouts  11.2 us (9%)
  waiting for transfers between devices  5.2 us (4%)
  other arithmetic  2.04 us (2%)
    all_to_all x1, blocking collectives, local(): lax.all_to_all(mine.reshape(groups * pieces, rows, rhs), ('z', 'narrow'),...  30.3 us
    all_to_all x1, blocking collectives, local(): sums = lax.all_to_all(sums, ('z', 'core', 'narrow'), 0, 0, tiled=True)  19.7 us
    all_to_all x1, blocking collectives, local(): packed = lax.all_to_all(copies, 'narrow', 0, 0, tiled=True)  11.4 us
    unnamed x44, local copies, waits for them, and re-layouts  9.56 us
    ppermute x1, starting transfers between devices, local(): halo = lax.ppermute(residual[0].astype(BF16), 'narrow', back)  5.76 us
    pallas_call x1, Pallas kernels, search_outer(): pl.pallas_call(outer_kernel, grid=(2,), in_specs=operators(nb, ni, lambda...  5.66 us
    pallas_call x1, Pallas kernels, search_inner(): pl.pallas_call(inner_kernel, grid=(subs - 2,), in_specs=operators(nb, ni,...  5.58 us
    ppermute x1, starting transfers between devices, local(): twin = lax.ppermute(ring, 'core', [(0, 1), (1, 0)])  5.18 us
  transfers between devices with their start and end apart: 10, of which 5 were waited for; matrix products, arithmetic and copies ran while one was open for 2% of the time, Pallas kernels for 9%

profile of v2, /device:TPU:1, one launch (start us, length us, event | category | flops | bytes accessed | tf_op | source)
XLA Modules:
  0.0 126.3 jit_solution(3077840590251878678)
XLA Ops:
  1.5 5.8 %collective-permute-start = (bf16[256,128]{1,0:T(8,128)(2,1)S(1)}, bf16[256,128]{1,0:T(8,128)(2,1)S(1)}, u32[]{:S(2)}, u32[]{:S(2)}) collective-permute-start(bf16[256,128]{1,0:T(8,128)(2,1)S(1)} %fusion), channel_id=1, source_target_pairs={{1,0},{2,1},{3,2},{4,3},{5,4},{6,5},{7,6},{8,7},{9,8},{10,9},{11,1... | collective-permute-start | bytes 196616 | tf_op jit(solution)/shard_map/ppermute | solution.py:584
  8.0 1.0 copy-done.1
  9.7 1.1 copy-done.14
  12.5 3.9 %place_panels.1 = (f32[4,640,128]{2,1,0:T(8,128)S(1)}, f32[4,640,128]{2,1,0:T(8,128)}, bf16[4,256,512]{2,1,0:T(8,128)(2,1)S(1)}) custom-call(s32[4]{0:T(128)S(1)} %bitcast.22, s32[4]{0:T(128)S(1)} %copy-done.16, s32[1]{0:T(128)} %bitcast.1.core, s32[4,1,200]{2,1,0:T(1,128)S(1)} %broadcast_in_dim.6.pm, bf16[4,200,512]{2,1,0:T(8,128)(2,1)S(1)} %bitcast.25, ...), custom_call_target="tpu_custom_call" | custom-call | flops 1000000000 | bytes 6000000 | tf_op jit(solution)/shard_map/place_panels/pallas_call | solution.py:83
  16.5 1.1 add_halo.1
  17.6 1.1 copy-done.5
  19.6 1.6 %collective-permute-start.2 = (f32[256,128]{1,0:T(8,128)S(1)}, f32[256,128]{1,0:T(8,128)S(1)}, u32[]{:S(2)}, u32[]{:S(2)}) collective-permute-start(f32[256,128]{1,0:T(8,128)S(1)} %slice_bitcast_fusion), channel_id=1, source_target_pairs={{1,0},{2,1},{3,2},{4,3},{5,4},{6,5},{7,6},{8,7},{9,8},{10,9},{11,1... | collective-permute-start | bytes 393224 | tf_op jit(solution)/shard_map/ppermute | solution.py:585
  21.2 1.4 %collective-permute-done.1 = f32[4,640,128]{2,1,0:T(8,128)} collective-permute-done((f32[4,640,128]{2,1,0:T(8,128)}, f32[4,640,128]{2,1,0:T(8,128)}, u32[]{:S(2)}, u32[]{:S(2)}) %collective-permute-start.1) | collective-permute-done | bytes 1310752 | tf_op jit(solution)/shard_map/ppermute | solution.py:592
  22.6 2.0 %add.9 = f32[4,640,128]{2,1,0:T(8,128)S(1)} add(f32[4,640,128]{2,1,0:T(8,128)} %copy-done.5, f32[4,640,128]{2,1,0:T(8,128)} %collective-permute-done.1) | non-fusion elementwise | flops 327680 | bytes 3932160 | tf_op jit(solution)/shard_map/add | solution.py:592
  24.8 30.3 %all_to_all.15.parts = f32[64,40,128]{2,1,0:T(8,128)S(1)} all-to-all(f32[64,40,128]{2,1,0:T(8,128)S(1)} %bitcast.26), channel_id=1, replica_groups=mesh['z'=4,'core'=2,'narrow'=16] {'z','narrow'}, dimensions={0} | all-to-all | bytes 2621440 | tf_op jit(solution)/shard_map/all_to_all | solution.py:595
  55.3 11.4 %all_to_all.16 = f32[16,40,128]{2,1,0:T(8,128)S(1)} all-to-all(f32[16,40,128]{2,1,0:T(8,128)S(1)} %sum_copies.1), channel_id=1, replica_groups=mesh['z'=4,'core'=2,'narrow'=16] {'narrow'}, dimensions={0} | all-to-all | bytes 655360 | tf_op jit(solution)/shard_map/all_to_all | solution.py:599
  66.6 4.2 %solve_block.1 = bf16[256,128]{1,0:T(8,128)(2,1)S(1)} custom-call(f32[640,128]{1,0:T(8,128)S(1)} %bitcast.20, f32[1,256,256]{2,1,0:T(8,128)S(1)} %copy-done.10), custom_call_target="tpu_custom_call" | custom-call | tf_op jit(solution)/shard_map/solve_block/pallas_call | solution.py:284
  74.0 1.7 %collective-permute-done.3 = bf16[256,128]{1,0:T(8,128)(2,1)S(1)} collective-permute-done((bf16[256,128]{1,0:T(8,128)(2,1)S(1)}, bf16[256,128]{1,0:T(8,128)(2,1)S(1)}, u32[]{:S(2)}, u32[]{:S(2)}) %collective-permute-start.3) | collective-permute-done | bytes 65568 | tf_op jit(solution)/shard_map/ppermute | solution.py:602
  75.8 1.2 collective-permute-done.4
  77.1 5.2 %collective-permute-start.6 = (bf16[4,256,128]{2,1,0:T(8,128)(2,1)S(1)}, bf16[4,256,128]{2,1,0:T(8,128)(2,1)S(1)}, u32[]{:S(2)}, u32[]{:S(2)}) collective-permute-start(bf16[4,256,128]{2,1,0:T(8,128)(2,1)S(1)} %pad_maximum_fusion.ring), channel_id=1, source_target_pairs={{0,16},{16,0},{1,17},{17,1},{2,18},{18,2},{3,19},{19,3},{4,20},{20... | collective-permute-start | bytes 786440 | tf_op jit(solution)/shard_map/ppermute | solution.py:604
  82.2 1.6 %copy-done.8 = bf16[4,512,512]{2,1,0:T(8,128)(2,1)S(1)} copy-done((bf16[4,512,512]{2,1,0:T(8,128)(2,1)S(1)}, bf16[4,512,512]{2,1,0:T(8,128)(2,1)}, u32[]{:S(2)}) %copy-start.8) | copy-done | bytes 2097176
  83.8 1.3 neumann_half.1
  85.1 1.6 %coarse_part.1 = (f32[4,512,128]{2,1,0:T(8,128)S(1)}, f32[256,128]{1,0:T(8,128)S(1)}, f32[256,128]{1,0:T(8,128)S(1)}) custom-call(s32[4]{0:T(128)S(1)} %compare_convert_fusion.other, s32[4]{0:T(128)S(1)} %and_select_fusion.turn, bf16[4,512,256]{2,1,0:T(8,128)(2,1)S(1)} %get-tuple-element.33.turned, bf16[4,256,128]{2,1,0:T(8,128)(2,1)S(1)} %pad_maximum_fusion.ring, ...), custom_call_target="tpu_custom_call" | custom-call | tf_op jit(solution)/shard_map/coarse_part/pallas_call | solution.py:356
  86.9 4.7 %collective-permute-start.8 = (f32[256,128]{1,0:T(8,128)S(1)}, f32[256,128]{1,0:T(8,128)S(1)}, u32[]{:S(2)}, u32[]{:S(2)}) collective-permute-start(f32[256,128]{1,0:T(8,128)S(1)} %get-tuple-element.37), channel_id=1, source_target_pairs={{1,0},{2,1},{3,2},{4,3},{5,4},{6,5},{7,6},{8,7},{9,8},{10,9},{11,1... | collective-permute-start | bytes 393224 | tf_op jit(solution)/shard_map/ppermute | solution.py:609
  91.6 2.3 %copy-done = bf16[4,512,1152]{2,1,0:T(8,128)(2,1)S(1)} copy-done((bf16[4,512,1152]{2,1,0:T(8,128)(2,1)S(1)}, bf16[4,512,1152]{2,1,0:T(8,128)(2,1)}, u32[]{:S(2)}) %copy-start) | copy-done | bytes 4718616
  93.9 5.6 %search_inner.1 = (f32[2,512,256]{2,1,0:T(8,128)S(1)}, f32[4,128]{1,0:T(4,128)S(1)}) custom-call(bf16[4,512,512]{2,1,0:T(8,128)(2,1)S(1)} %copy-done.3, bf16[4,512,1152]{2,1,0:T(8,128)(2,1)S(1)} %copy-done, bf16[4,1152,1152]{2,1,0:T(8,128)(2,1)S(1)} %bitcast.17, f32[4,512,128]{2,1,0:T(8,128)S(1)} %get-tuple-element.35.pre, f32[4,256,128]{2,1,0:T(8,128)S(1)} %copy-done.4, ...), custom_call_target="tpu_custom_call" | custom-call | flops 2835349504 | bytes 8716288 | tf_op jit(solution)/shard_map/search_inner/pallas_call | solution.py:489
  99.6 5.7 %search_outer.1 = (f32[2,512,256]{2,1,0:T(8,128)S(1)}, f32[128,4,128]{2,1,0:T(4,128)S(1)}, f32[256,256]{1,0:T(8,128)S(1)}) custom-call(bf16[4,512,512]{2,1,0:T(8,128)(2,1)S(1)} %copy-done.3, bf16[4,512,1152]{2,1,0:T(8,128)(2,1)S(1)} %bitcast.19, bf16[4,1152,1152]{2,1,0:T(8,128)(2,1)S(1)} %bitcast.17, f32[4,512,128]{2,1,0:T(8,128)S(1)} %get-tuple-element.35.pre, ...), custom_call_target="tpu_custom_call" | custom-call | flops 2835349504 | bytes 8716288 | tf_op jit(solution)/shard_map/search_outer/pallas_call | solution.py:507
  105.3 19.7 %all_to_all.17.sums = f32[128,4,128]{2,1,0:T(4,128)S(1)} all-to-all(f32[128,4,128]{2,1,0:T(4,128)S(1)} %get-tuple-element.40), channel_id=1, replica_groups=mesh['z'=4,'core'=2,'narrow'=16] {'z','core','narrow'}, dimensions={0} | all-to-all | bytes 524288 | tf_op jit(solution)/shard_map/all_to_all | solution.py:625
  125.0 1.3 %update.1 = (f32[4,256,128]{2,1,0:T(8,128)}, f32[4,256,128]{2,1,0:T(8,128)}) custom-call(f32[128,4,128]{2,1,0:T(4,128)S(1)} %all_to_all.17.sums, f32[1,128]{1,0:T(1,128)S(1)} %bitcast.24, f32[4,512,128]{2,1,0:T(8,128)S(1)} %get-tuple-element.35.pre, f32[256,128]{1,0:T(8,128)S(1)} %collective-permute-done.7.from_prev, ...), custom_call_target="tpu_custom_call" | custom-call | tf_op jit(solution)/shard_map/update/pallas_call | solution.py:553
  (61 shorter events, 8.8 us)
Async XLA Ops:
  1.5 14.9 %collective-permute-start = (bf16[256,128]{1,0:T(8,128)(2,1)S(1)}, bf16[256,128]{1,0:T(8,128)(2,1)S(1)}, u32[]{:S(2)}, u32[]{:S(2)}) collective-permute-start(bf16[256,128]{1,0:T(8,128)(2,1)S(1)} %fusion), channel_id=1, source_target_pairs={{1,0},{2,1},{3,2},{4,3},{5,4},{6,5},{7,6},{8,7},{9,8},{10,9},{11,1... | collective-permute-start | bytes 196616 | tf_op jit(solution)/shard_map/ppermute | solution.py:584
  12.5 79.1 %slice-start = ((s8[10616832]{0:T(1024)(128)(4,1)}), s8[2228224]{0:T(1024)(128)(4,1)S(1)}, s32[]{:S(2)}) async-start(s8[10616832]{0:T(1024)(128)(4,1)} %bitcast.16), calls=%async_computation.3 | async-start | bytes 4456448
  16.4 3.2 %copy-start.4 = (f32[4,256,128]{2,1,0:T(8,128)S(1)}, f32[4,256,128]{2,1,0:T(8,128)}, u32[]{:S(2)}) copy-start(f32[4,256,128]{2,1,0:T(8,128)} %direction.5) | copy-start | bytes 1572868
  16.5 4.7 %copy-start.12 = (s32[4,1]{0,1:T(1,128)S(1)}, s32[4,1]{0,1:T(1,128)}, u32[]{:S(2)}) copy-start(s32[4,1]{0,1:T(1,128)} %param.25) | copy-start | bytes 52
  18.6 4.0 %collective-permute-start.1 = (f32[4,640,128]{2,1,0:T(8,128)}, f32[4,640,128]{2,1,0:T(8,128)}, u32[]{:S(2)}, u32[]{:S(2)}) collective-permute-start(f32[4,640,128]{2,1,0:T(8,128)} %get-tuple-element.27), channel_id=1, source_target_pairs={{0,16},{16,0},{1,17},{17,1},{2,18},{18,2},{3,19},{19,3},{4,20},{20... | collective-permute-start | bytes 3932168 | tf_op jit(solution)/shard_map/ppermute | solution.py:592
  19.6 47.0 %copy-start.10 = (f32[1,256,256]{2,1,0:T(8,128)S(1)}, f32[1,256,256]{2,1,0:T(8,128)}, u32[]{:S(2)}) copy-start(f32[1,256,256]{2,1,0:T(8,128)} %base.1) | copy-start | bytes 786436
  19.6 5.2 %collective-permute-start.2 = (f32[256,128]{1,0:T(8,128)S(1)}, f32[256,128]{1,0:T(8,128)S(1)}, u32[]{:S(2)}, u32[]{:S(2)}) collective-permute-start(f32[256,128]{1,0:T(8,128)S(1)} %slice_bitcast_fusion), channel_id=1, source_target_pairs={{1,0},{2,1},{3,2},{4,3},{5,4},{6,5},{7,6},{8,7},{9,8},{10,9},{11,1... | collective-permute-start | bytes 393224 | tf_op jit(solution)/shard_map/ppermute | solution.py:585
  22.6 69.0 %slice-start.1 = ((s8[10616832]{0:T(1024)(128)(4,1)}), s8[4194304]{0:T(1024)(128)(4,1)S(1)}, s32[]{:S(2)}) async-start(s8[10616832]{0:T(1024)(128)(4,1)} %bitcast.16), calls=%async_computation.4 | async-start | bytes 8388608
  24.8 74.7 %slice-start.3 = ((s8[4718592]{0:T(1024)(128)(4,1)}), s8[4194304]{0:T(1024)(128)(4,1)S(1)}, s32[]{:S(2)}) async-start(s8[4718592]{0:T(1024)(128)(4,1)} %bitcast.18), calls=%async_computation.6 | async-start | bytes 8388608
  55.1 27.1 %copy-start.2 = (f32[4,256,128]{2,1,0:T(8,128)S(1)}, f32[4,256,128]{2,1,0:T(8,128)}, u32[]{:S(2)}) copy-start(f32[4,256,128]{2,1,0:T(8,128)} %residual.5) | copy-start | bytes 1572868
  55.1 27.1 %copy-start.7 = (bf16[4,256,512]{2,1,0:T(8,128)(2,1)S(1)}, bf16[4,256,512]{2,1,0:T(8,128)(2,1)}, u32[]{:S(2)}) copy-start(bf16[4,256,512]{2,1,0:T(8,128)(2,1)} %copy-done.6) | copy-start | bytes 3145732
  55.2 36.3 %slice-start.2 = ((s8[10616832]{0:T(1024)(128)(4,1)}), s8[4194304]{0:T(1024)(128)(4,1)S(1)}, s32[]{:S(2)}) async-start(s8[10616832]{0:T(1024)(128)(4,1)} %bitcast.16), calls=%async_computation.5 | async-start | bytes 8388608
  70.9 3.2 %collective-permute-start.5 = (bf16[256,128]{1,0:T(8,128)(2,1)S(1)}, bf16[256,128]{1,0:T(8,128)(2,1)S(1)}, u32[]{:S(2)}, u32[]{:S(2)}) collective-permute-start(bf16[256,128]{1,0:T(8,128)(2,1)S(1)} %solve_block.1), channel_id=1, source_target_pairs={{0,96},{32,0},{64,32},{96,64},{1,97},{33,1},{65,33},{97,65},{2,98}... | collective-permute-start | bytes 196616 | tf_op jit(solution)/shard_map/ppermute | solution.py:602
  71.5 4.3 %collective-permute-start.3 = (bf16[256,128]{1,0:T(8,128)(2,1)S(1)}, bf16[256,128]{1,0:T(8,128)(2,1)S(1)}, u32[]{:S(2)}, u32[]{:S(2)}) collective-permute-start(bf16[256,128]{1,0:T(8,128)(2,1)S(1)} %solve_block.1), channel_id=1, source_target_pairs={{0,32},{32,64},{64,96},{96,0},{1,33},{33,65},{65,97},{97,1},{2,34}... | collective-permute-start | bytes 196616 | tf_op jit(solution)/shard_map/ppermute | solution.py:602
  72.4 4.6 %collective-permute-start.4 = (bf16[256,128]{1,0:T(8,128)(2,1)S(1)}, bf16[256,128]{1,0:T(8,128)(2,1)S(1)}, u32[]{:S(2)}, u32[]{:S(2)}) collective-permute-start(bf16[256,128]{1,0:T(8,128)(2,1)S(1)} %solve_block.1), channel_id=1, source_target_pairs={{0,64},{32,96},{64,0},{96,32},{1,65},{33,97},{65,1},{97,33},{2,66}... | collective-permute-start | bytes 196616 | tf_op jit(solution)/shard_map/ppermute | solution.py:602
  77.1 8.0 %collective-permute-start.6 = (bf16[4,256,128]{2,1,0:T(8,128)(2,1)S(1)}, bf16[4,256,128]{2,1,0:T(8,128)(2,1)S(1)}, u32[]{:S(2)}, u32[]{:S(2)}) collective-permute-start(bf16[4,256,128]{2,1,0:T(8,128)(2,1)S(1)} %pad_maximum_fusion.ring), channel_id=1, source_target_pairs={{0,16},{16,0},{1,17},{17,1},{2,18},{18,2},{3,19},{19,3},{4,20},{20... | collective-permute-start | bytes 786440 | tf_op jit(solution)/shard_map/ppermute | solution.py:604
  85.1 6.5 %copy-start.3 = (bf16[4,512,512]{2,1,0:T(8,128)(2,1)S(1)}, bf16[4,512,512]{2,1,0:T(8,128)(2,1)}, u32[]{:S(2)}) copy-start(bf16[4,512,512]{2,1,0:T(8,128)(2,1)} %stiffness.3) | copy-start | bytes 6291460
  86.7 12.8 %collective-permute-start.7 = (f32[256,128]{1,0:T(8,128)S(1)}, f32[256,128]{1,0:T(8,128)S(1)}, u32[]{:S(2)}, u32[]{:S(2)}) collective-permute-start(f32[256,128]{1,0:T(8,128)S(1)} %get-tuple-element.36), channel_id=1, source_target_pairs={{0,1},{1,2},{2,3},{3,4},{4,5},{5,6},{6,7},{7,8},{8,9},{9,10},{10,1... | collective-permute-start | bytes 393224 | tf_op jit(solution)/shard_map/ppermute | solution.py:608
  86.9 12.6 %collective-permute-start.8 = (f32[256,128]{1,0:T(8,128)S(1)}, f32[256,128]{1,0:T(8,128)S(1)}, u32[]{:S(2)}, u32[]{:S(2)}) collective-permute-start(f32[256,128]{1,0:T(8,128)S(1)} %get-tuple-element.37), channel_id=1, source_target_pairs={{1,0},{2,1},{3,2},{4,3},{5,4},{6,5},{7,6},{8,7},{9,8},{10,9},{11,1... | collective-permute-start | bytes 393224 | tf_op jit(solution)/shard_map/ppermute | solution.py:609
  91.6 2.3 %copy-start = (bf16[4,512,1152]{2,1,0:T(8,128)(2,1)S(1)}, bf16[4,512,1152]{2,1,0:T(8,128)(2,1)}, u32[]{:S(2)}) copy-start(bf16[4,512,1152]{2,1,0:T(8,128)(2,1)} %coupling.3) | copy-start | bytes 14155780
  93.9 5.6 %slice-start.4 = ((s8[4718592]{0:T(1024)(128)(4,1)}), s8[524288]{0:T(1024)(128)(4,1)S(1)}, s32[]{:S(2)}) async-start(s8[4718592]{0:T(1024)(128)(4,1)} %bitcast.18), calls=%async_computation.7 | async-start | bytes 1048576
  99.6 25.4 %copy-start.9 = (f32[4,256,128]{2,1,0:T(8,128)S(1)}, f32[4,256,128]{2,1,0:T(8,128)}, u32[]{:S(2)}) copy-start(f32[4,256,128]{2,1,0:T(8,128)} %solution.1) | copy-start | bytes 1572868
  99.6 25.4 %copy-start.13 = (f32[128]{0:T(128)S(1)}, f32[128]{0:T(128)}, u32[]{:S(2)}) copy-start(f32[128]{0:T(128)} %param.17) | copy-start | bytes 1540
  105.2 19.7 %collective-permute-start.9 = (f32[256,256]{1,0:T(8,128)S(1)}, f32[256,256]{1,0:T(8,128)S(1)}, u32[]{:S(2)}, u32[]{:S(2)}) collective-permute-start(f32[256,256]{1,0:T(8,128)S(1)} %get-tuple-element.43), channel_id=1, source_target_pairs={{0,1},{1,2},{2,3},{3,4},{4,5},{5,6},{6,7},{7,8},{8,9},{9,10},{10,1... | collective-permute-start | bytes 786440 | tf_op jit(solution)/shard_map/ppermute | solution.py:624
  (8 other events, 8.3 us)

commit v3 on v2

--- a/solution.py
+++ b/solution.py
@@ -12,6 +12,8 @@
 TN = (((0,), (0,)), ((), ()))
 SMALL = 16 * 1024 * 1024
 LARGE = 24 * 1024 * 1024
+INNER = 24 * 1024 * 1024
+PLACE = 16 * 1024 * 1024
 HIGHEST = lax.Precision.HIGHEST
 
 
@@ -31,48 +33,54 @@
     return pltpu.CompilerParams(vmem_limit_bytes=limit)
 
 
+def stay(*arrays):
+    return tuple(pltpu.with_memory_space_constraint(x, pltpu.HBM) for x in arrays)
+
+
 def column_sum(value):
     return jnp.sum(value, axis=0, keepdims=True)
 
 
-def place_kernel(own, chg, core, pm, basis, panel, res, keep, send, spread):
+def chosen(pm, s, co):
+    rows = lax.broadcasted_iota(jnp.int32, (co, pm.shape[1]), 0)
+    return (rows == pm[pl.ds(s, 1)]).astype(F32).astype(BF16)
+
+
+def place_kernel(own, chg, core, pm, basis, panel, res, keep, send, edge, held, sems):
     s = pl.program_id(0)
-    co = spread.shape[1]
+    last = pl.num_programs(0) - 1
+    co = edge.shape[0]
     half = co // 2
     face = res.shape[1]
 
     @pl.when(s == 0)
     def _():
-        keep[...] = jnp.zeros_like(keep)
-        send[...] = jnp.zeros_like(send)
-
-    rows = lax.broadcasted_iota(jnp.int32, (co, pm.shape[2]), 0)
-    select = (rows == pm[0]).astype(F32).astype(BF16)
+        held[...] = jnp.zeros_like(held)
+
+    select = chosen(pm, s, co)
     wide_basis = dot(select, basis[0]).astype(BF16)
-    spread[0] = wide_basis
     placed = dot(dot(select, panel[0]).astype(BF16), select, NT) * chg[s].astype(F32)
-    last = pl.num_programs(0) - 1
     here = res[s].astype(BF16)
     there = res[jnp.minimum(s + 1, last)].astype(BF16)
     rhs = dot(wide_basis[:, :face], here)
     rhs += jnp.where(s < last, dot(wide_basis[:, face:], there), 0.0)
     owner = own[s]
     place = owner >> 1
-    other = (owner & 1) != core[0]
-
-    def add(to):
-        to[place, 0:half] += placed[:half, :half]
-        to[place, half:co] += placed[half:, :half]
-        to[place, co : co + half] += placed[half:, half:]
-        to[place, co + half :] += rhs
-
-    @pl.when(other)
-    def _():
-        add(send)
-
-    @pl.when(jnp.logical_not(other))
-    def _():
-        add(keep)
+    leaves = (owner & 1) ^ core[0]
+    held[leaves, place, 0:half] += placed[:half, :half]
+    held[leaves, place, half:co] += placed[half:, :half]
+    held[leaves, place, co : co + half] += placed[half:, half:]
+    held[leaves, place, co + half :] += rhs
+
+    @pl.when(s == last)
+    def _():
+        edge[...] = wide_basis[:, face:]
+        first = pltpu.make_async_copy(held.at[1], send, sems.at[0])
+        second = pltpu.make_async_copy(held.at[0], keep, sems.at[1])
+        first.start()
+        second.start()
+        first.wait()
+        second.wait()
 
 
 def place_panels(own, chg, core, prim_map, basis, panels, residual, groups):
@@ -80,6 +88,7 @@
     co = 2 * residual.shape[2]
     rows = 3 * (co // 2) + co
     packed = (groups, rows, co // 2)
+    hbm = pl.BlockSpec(memory_space=pl.ANY)
     return pl.pallas_call(
         place_kernel,
         grid=(subs,),
@@ -87,24 +96,25 @@
             smem(),
             smem(),
             smem(),
-            pl.BlockSpec((1, 1, npr), lambda s: (s, 0, 0)),
+            whole((subs, npr)),
             pl.BlockSpec((1, npr, nb), lambda s: (s, 0, 0)),
             pl.BlockSpec((1, npr, npr), lambda s: (s, 0, 0)),
             whole(residual.shape),
         ],
-        out_specs=[whole(packed), whole(packed), pl.BlockSpec((1, co, nb), lambda s: (s, 0, 0))],
+        out_specs=[hbm, hbm, whole((co, nb // 2))],
         out_shape=[
             jax.ShapeDtypeStruct(packed, F32),
             jax.ShapeDtypeStruct(packed, F32),
-            jax.ShapeDtypeStruct((subs, co, nb), BF16),
-        ],
-        compiler_params=params(),
+            jax.ShapeDtypeStruct((co, nb // 2), BF16),
+        ],
+        scratch_shapes=[pltpu.VMEM((2,) + packed, F32), pltpu.SemaphoreType.DMA((2,))],
+        compiler_params=params(PLACE),
         cost_estimate=pl.CostEstimate(flops=10**9, bytes_accessed=6 * 10**6, transcendentals=0),
         name="place_panels",
-    )(own, chg, core, prim_map, basis, panels, residual)
-
-
-def halo_kernel(own, core, spread, halo, keep_in, send_in, keep, send, held, sem):
+    )(*stay(own, chg), core, *stay(prim_map, basis, panels, residual))
+
+
+def halo_kernel(own, core, edge, halo, keep_in, send_in, keep, send, held, sem):
     del keep_in, send_in
     owner = own[own.shape[0] - 1]
     place = owner >> 1
@@ -115,7 +125,7 @@
         part = to.at[place, pl.ds(to.shape[1] - rows, rows)]
         fetch = pltpu.make_async_copy(part, held, sem)
         fetch.start()
-        value = dot(spread[0], halo[...])
+        value = dot(edge[...], halo[...])
         fetch.wait()
         held[...] += value
         put = pltpu.make_async_copy(held, part, sem)
@@ -131,8 +141,7 @@
         add(keep)
 
 
-def add_halo(own, core, spread, halo, keep, send):
-    subs, co, nb = spread.shape
+def add_halo(own, core, edge, halo, keep, send):
     hbm = pl.BlockSpec(memory_space=pl.ANY)
     return pl.pallas_call(
         halo_kernel,
@@ -140,7 +149,7 @@
         in_specs=[
             smem(),
             smem(),
-            pl.BlockSpec((1, co, nb // 2), lambda _: (subs - 1, 0, 1)),
+            whole(edge.shape),
             whole(halo.shape),
             hbm,
             hbm,
@@ -148,10 +157,10 @@
         out_specs=[hbm, hbm],
         out_shape=[jax.ShapeDtypeStruct(keep.shape, F32), jax.ShapeDtypeStruct(send.shape, F32)],
         input_output_aliases={4: 0, 5: 1},
-        scratch_shapes=[pltpu.VMEM((co, halo.shape[1]), F32), pltpu.SemaphoreType.DMA],
-        compiler_params=params(),
+        scratch_shapes=[pltpu.VMEM((edge.shape[0], halo.shape[1]), F32), pltpu.SemaphoreType.DMA],
+        compiler_params=params(PLACE),
         name="add_halo",
-    )(own, core, spread, halo, keep, send)
+    )(own, core, edge, halo, keep, send)
 
 
 def gather_kernel(parts, out):
@@ -296,24 +305,26 @@
     )(packed, base)
 
 
-def neumann_kernel(neumann, spread, res, halo, out, turned):
+def neumann_kernel(pm, neumann, basis, res, halo, out, turned):
     s = pl.program_id(0)
     last = pl.num_programs(0) - 1
     here = res[s].astype(BF16)
     there = jnp.where(s < last, res[jnp.minimum(s + 1, last)], halo[...].astype(F32)).astype(BF16)
     out[0] = 0.5 * dot(neumann[0], jnp.concatenate([here, there], axis=0))
-    turned[0] = spread[0].T
-
-
-def neumann_half(neumann, spread, residual, halo):
-    subs, co, nb = spread.shape
+    turned[0] = dot(chosen(pm, s, turned.shape[2]), basis[0]).astype(BF16).T
+
+
+def neumann_half(prim_map, neumann, basis, residual, halo):
+    subs, npr, nb = basis.shape
     rhs = residual.shape[2]
+    co = 2 * rhs
     return pl.pallas_call(
         neumann_kernel,
         grid=(subs,),
         in_specs=[
+            whole((subs, npr)),
             pl.BlockSpec((1, nb, nb), lambda s: (s, 0, 0)),
-            pl.BlockSpec((1, co, nb), lambda s: (s, 0, 0)),
+            pl.BlockSpec((1, npr, nb), lambda s: (s, 0, 0)),
             whole(residual.shape),
             whole(halo.shape),
         ],
@@ -330,14 +341,15 @@
             flops=2 * subs * nb * nb * rhs, bytes_accessed=4 * 10**6, transcendentals=0
         ),
         name="neumann_half",
-    )(neumann, spread, residual, halo)
-
-
-def coarse_kernel(other, turn, turned, ring, twin, part, out, near, far):
+    )(*stay(prim_map, neumann, basis), residual, halo)
+
+
+def coarse_kernel(own, core, z, turned, ring, twin, part, out, near, far):
     s = pl.program_id(0)
-    face = near.shape[0]
-    at = turn[s]
-    solved = jnp.where(other[s] == 1, twin[at].astype(F32), ring[at].astype(F32)).astype(BF16)
+    face = far.shape[0]
+    groups = ring.shape[0]
+    at = lax.rem(z[0] - (own[s] >> 1) + groups, groups)
+    solved = jnp.where((own[s] & 1) != core[0], twin[at].astype(F32), ring[at].astype(F32)).astype(BF16)
     found = part[0] + 0.5 * dot(turned[0], solved)
     out[0] = found
 
@@ -350,13 +362,14 @@
         far[...] = found[face:]
 
 
-def coarse_part(other, turn, turned, ring, twin, part):
+def coarse_part(own, core, z, turned, ring, twin, part):
     subs, nb, co = turned.shape
     rhs = ring.shape[2]
     return pl.pallas_call(
         coarse_kernel,
         grid=(subs,),
         in_specs=[
+            smem(),
             smem(),
             smem(),
             pl.BlockSpec((1, nb, co), lambda s: (s, 0, 0)),
@@ -376,13 +389,14 @@
         ],
         compiler_params=params(),
         name="coarse_part",
-    )(other, turn, turned, ring, twin, part)
+    )(own, core, z, turned, ring, twin, part)
 
 
 def action(stiffness, coupling, interior, field):
-    load = dot(coupling, field, TN).astype(BF16)
-    inside = dot(interior, load).astype(BF16)
-    return dot(stiffness, field) - dot(coupling, inside)
+    across = field.T.astype(BF16)
+    load = dot(across, coupling).astype(BF16)
+    inside = dot(load, interior, NT).astype(BF16)
+    return dot(stiffness, field.astype(BF16)) - dot(coupling, inside, NT)
 
 
 def operators(nb, ni, place):
@@ -406,7 +420,7 @@
     field = jnp.concatenate(
         [jnp.concatenate([own_p, own_d], axis=1), jnp.concatenate([far_p, far_d], axis=1)], axis=0
     )
-    both = action(stiffness[0], coupling[0], interior[0], field.astype(BF16))
+    both = action(stiffness[0], coupling[0], interior[0], field)
     image, moved = both[:, :rhs], both[:, rhs:]
     parts = jnp.concatenate(
         [
@@ -495,10 +509,10 @@
             jax.ShapeDtypeStruct((subs - 2, nb, 2 * rhs), F32),
             jax.ShapeDtypeStruct((4, rhs), F32),
         ],
-        compiler_params=params(LARGE),
+        compiler_params=params(INNER),
         cost_estimate=cost(subs - 2, nb, ni, 2 * rhs),
         name="search_inner",
-    )(stiffness, coupling, interior, *rest)
+    )(*stay(stiffness, coupling, interior), *rest)
 
 
 def search_outer(devices, stiffness, coupling, interior, *rest):
@@ -522,7 +536,7 @@
         compiler_params=params(LARGE),
         cost_estimate=cost(2, nb, ni, 2 * rhs),
         name="search_outer",
-    )(stiffness, coupling, interior, *rest)
+    )(*stay(stiffness, coupling, interior), *rest)
 
 
 def update_kernel(
@@ -580,18 +594,14 @@
     own = owners[:, 0]
     core = lax.axis_index("core")
     core_ref = core.astype(jnp.int32).reshape(1)
+    z_ref = lax.axis_index("z").astype(jnp.int32).reshape(1)
 
     halo = lax.ppermute(residual[0].astype(BF16), "narrow", back)
-    direction_halo = lax.ppermute(direction[0], "narrow", back)
-    other = ((own & 1) != core).astype(jnp.int32)
-    turn = ((lax.axis_index("z") - (own >> 1)) % groups).astype(jnp.int32)
-    keep, send, spread = place_panels(
-        own, changed, core_ref, prim_map[:, None, :], jnp.swapaxes(basis, 1, 2), panels, residual, groups
-    )
-    keep, send = add_halo(own, core_ref, spread, halo, keep, send)
+    basis = jnp.swapaxes(basis, 1, 2)
+    keep, send, edge = place_panels(own, changed, core_ref, prim_map, basis, panels, residual, groups)
+    keep, send = add_halo(own, core_ref, edge, halo, keep, send)
     mine = keep + lax.ppermute(send, "core", [(0, 1), (1, 0)])
     rows = mine.shape[1] // pieces
-    mine, direction_halo, other, turn = lax.optimization_barrier((mine, direction_halo, other, turn))
     parts = lax.all_to_all(
         mine.reshape(groups * pieces, rows, rhs), ("z", "narrow"), 0, 0, tiled=True
     )
@@ -600,11 +610,13 @@
     solved = solve_block(packed.reshape(pieces * rows, rhs), base_coarse)
 
     turns = [lax.ppermute(solved, "z", [(i, (i + d) % groups) for i in range(groups)]) for d in range(1, groups)]
+    given, heading, _ = lax.optimization_barrier((residual, direction[0], solved))
+    direction_halo = lax.ppermute(heading, "narrow", back)
+    part, turned = neumann_half(prim_map, neumann, basis, given, halo)
+    turns, part, turned = lax.optimization_barrier((turns, part, turned))
     ring = jnp.stack([solved] + turns)
     twin = lax.ppermute(ring, "core", [(0, 1), (1, 0)])
-    given, spread, _ = lax.optimization_barrier((residual, spread, solved))
-    part, turned = neumann_half(neumann, spread, given, halo)
-    pre, near, far = coarse_part(other, turn, turned, ring, twin, part)
+    pre, near, far = coarse_part(own, core_ref, z_ref, turned, ring, twin, part)
     from_prev = lax.ppermute(far, "narrow", forward)
     from_next = lax.ppermute(near, "narrow", back)
     inside, sums = search_inner(stiffness, coupling, interior, pre, direction, residual)

time: 127 us -> 114 us (0.90)
  local copies, waits for them, and re-layouts: 11.2 us -> 0.95 us
  Pallas kernels: 24.8 us -> 28.9 us
  waiting for transfers between devices: 5.2 us -> 2.95 us
  blocking collectives: 61.3 us -> 59.3 us
  other arithmetic: 2.04 us -> 0.17 us
    unnamed x44 -> x12, local copies, waits for them, and re-layouts: 9.56 us -> 0.03 us
    ppermute x3, waiting for transfers between devices: 3.58 us -> 0.01 us  [local(): lax.ppermute(solved, 'z', [(i, (i + d) % groups) for i in range(groups)])]
    pallas_call x3, Pallas kernels: 3.91 us -> 6.68 us  [the longest x1 3.59 us: neumann_half(): pl.pallas_call(neumann_kernel, grid=(subs,), in_specs=[whole((subs, npr))...]
    add x1, other arithmetic: 1.99 us -> 0.13 us  [local(): mine = keep + lax.ppermute(send, 'core', [(0, 1), (1, 0)])]
    all_to_all x1, blocking collectives: 30.3 us -> 28.8 us  [local(): lax.all_to_all(mine.reshape(groups * pieces, rows, rhs), ('z', 'narrow'),...]
  transfers between devices with their start and end apart: 10 -> 10, of which waited for: 5 -> 2; matrix products, arithmetic and copies ran while one was open for 2% -> 0% of each run, Pallas kernels for 9% -> 14%
where the time goes in v3:
time: 114 us; the launch traced here: 113 us
  blocking collectives  59.3 us (52%)
  Pallas kernels  28.9 us (25%)
  starting transfers between devices  20.2 us (18%)
  waiting for transfers between devices  2.95 us (3%)
    all_to_all x1, blocking collectives, local(): lax.all_to_all(mine.reshape(groups * pieces, rows, rhs), ('z', 'narrow'),...  28.8 us
    all_to_all x1, blocking collectives, local(): sums = lax.all_to_all(sums, ('z', 'core', 'narrow'), 0, 0, tiled=True)  19.3 us
    all_to_all x1, blocking collectives, local(): packed = lax.all_to_all(copies, 'narrow', 0, 0, tiled=True)  11.2 us
    pallas_call x1, Pallas kernels, search_outer(): pl.pallas_call(outer_kernel, grid=(2,), in_specs=operators(nb, ni, lambda...  6.29 us
    pallas_call x1, Pallas kernels, search_inner(): pl.pallas_call(inner_kernel, grid=(subs - 2,), in_specs=operators(nb, ni,...  6.15 us
    ppermute x1, starting transfers between devices, local(): halo = lax.ppermute(residual[0].astype(BF16), 'narrow', back)  5.76 us
    ppermute x1, starting transfers between devices, local(): from_next = lax.ppermute(near, 'narrow', back)  4.6 us
    ppermute x1, starting transfers between devices, local(): twin = lax.ppermute(ring, 'core', [(0, 1), (1, 0)])  4.34 us
  transfers between devices with their start and end apart: 10, of which 2 were waited for; matrix products, arithmetic and copies ran while one was open for 0% of the time, Pallas kernels for 14%

profile of v3, /device:TPU:1, one launch (start us, length us, event | category | flops | bytes accessed | tf_op | source)
XLA Modules:
  0.0 113.4 jit_solution(3691851256562787868)
XLA Ops:
  0.6 0.9 fusion
  1.5 5.8 %collective-permute-start = (bf16[256,128]{1,0:T(8,128)(2,1)S(1)}, bf16[256,128]{1,0:T(8,128)(2,1)S(1)}, u32[]{:S(2)}, u32[]{:S(2)}) collective-permute-start(bf16[256,128]{1,0:T(8,128)(2,1)S(1)} %fusion), channel_id=1, source_target_pairs={{1,0},{2,1},{3,2},{4,3},{5,4},{6,5},{7,6},{8,7},{9,8},{10,9},{11,1... | collective-permute-start | bytes 196616 | tf_op jit(solution)/shard_map/ppermute | solution.py:599
  7.3 4.2 %place_panels.1 = (f32[4,640,128]{2,1,0:T(8,128)S(1)}, f32[4,640,128]{2,1,0:T(8,128)S(1)}, bf16[256,256]{1,0:T(8,128)(2,1)S(1)}) custom-call(s32[4]{0:T(128)} %bitcast.17, s32[4]{0:T(128)} %chg.1, s32[1]{0:T(128)} %bitcast.1.core, s32[4,200]{1,0:T(4,128)} %pm.3, bf16[4,200,512]{2,1,0:T(8,128)(2,1)} %bitcast.22, bf16[4,200,200]{2,1,0:T(8,128)(2,1)} %panel.1, ...), custom_call_target="tpu_custom_call" | custom-call | flops 1000000000 | bytes 6000000 | tf_op jit(solution)/shard_map/place_panels/pallas_call | solution.py:92
  11.5 1.1 add_halo.1
  12.6 1.0 collective-permute-start.1
  13.6 2.7 %collective-permute-done.1 = f32[4,640,128]{2,1,0:T(8,128)S(1)} collective-permute-done((f32[4,640,128]{2,1,0:T(8,128)S(1)}, f32[4,640,128]{2,1,0:T(8,128)S(1)}, u32[]{:S(2)}, u32[]{:S(2)}) %collective-permute-start.1) | collective-permute-done | bytes 1310752 | tf_op jit(solution)/shard_map/ppermute | solution.py:603
  16.3 0.1 add.3
  16.4 28.8 %all_to_all.15.parts = f32[64,40,128]{2,1,0:T(8,128)S(1)} all-to-all(f32[64,40,128]{2,1,0:T(8,128)S(1)} %bitcast.21), channel_id=1, replica_groups=mesh['z'=4,'core'=2,'narrow'=16] {'z','narrow'}, dimensions={0} | all-to-all | bytes 2621440 | tf_op jit(solution)/shard_map/all_to_all | solution.py:605
  45.4 11.2 %all_to_all.16 = f32[16,40,128]{2,1,0:T(8,128)S(1)} all-to-all(f32[16,40,128]{2,1,0:T(8,128)S(1)} %sum_copies.1), channel_id=1, replica_groups=mesh['z'=4,'core'=2,'narrow'=16] {'narrow'}, dimensions={0} | all-to-all | bytes 655360 | tf_op jit(solution)/shard_map/all_to_all | solution.py:609
  56.5 4.2 %solve_block.1 = bf16[256,128]{1,0:T(8,128)(2,1)S(1)} custom-call(f32[640,128]{1,0:T(8,128)S(1)} %bitcast.15, f32[1,256,256]{2,1,0:T(8,128)S(1)} %copy-done.3), custom_call_target="tpu_custom_call" | custom-call | tf_op jit(solution)/shard_map/solve_block/pallas_call | solution.py:293
  60.8 0.2 collective-permute-start.2
  61.0 1.0 collective-permute-start.3
  61.9 2.0 %collective-permute-start.4 = (bf16[256,128]{1,0:T(8,128)(2,1)S(1)}, bf16[256,128]{1,0:T(8,128)(2,1)S(1)}, u32[]{:S(2)}, u32[]{:S(2)}) collective-permute-start(bf16[256,128]{1,0:T(8,128)(2,1)S(1)} %solve_block.1), channel_id=1, source_target_pairs={{0,96},{32,0},{64,32},{96,64},{1,97},{33,1},{65,33},{97,65},{2,98}... | collective-permute-start | bytes 196616 | tf_op jit(solution)/shard_map/ppermute | solution.py:612
  63.9 3.6 %neumann_half.1 = (f32[4,512,128]{2,1,0:T(8,128)S(1)}, bf16[4,512,256]{2,1,0:T(8,128)(2,1)S(1)}) custom-call(s32[4,200]{1,0:T(4,128)} %pm.3, bf16[4,512,512]{2,1,0:T(8,128)(2,1)} %neumann.1, bf16[4,200,512]{2,1,0:T(8,128)(2,1)} %bitcast.23, f32[4,256,128]{2,1,0:T(8,128)S(1)} %copy-done, bf16[256,128]{1,0:T(8,128)(2,1)S(1)} %collective-permute-done.halo), custom_call_target="tpu_custom_call" | custom-call | flops 268435456 | bytes 4000000 | tf_op jit(solution)/shard_map/neumann_half/pallas_call | solution.py:321
  67.6 4.3 %collective-permute-start.5 = (bf16[4,256,128]{2,1,0:T(8,128)(2,1)S(1)}, bf16[4,256,128]{2,1,0:T(8,128)(2,1)}, u32[]{:S(2)}, u32[]{:S(2)}) collective-permute-start(bf16[4,256,128]{2,1,0:T(8,128)(2,1)S(1)} %pad_maximum_fusion.ring), channel_id=1, source_target_pairs={{0,16},{16,0},{1,17},{17,1},{2,18},{18,2},{3,19},{19,3},{4,20},{20... | collective-permute-start | bytes 786440 | tf_op jit(solution)/shard_map/ppermute | solution.py:618
  72.0 1.0 collective-permute-start.8
  73.0 0.3 collective-permute-done.5.twin
  73.2 2.0 %coarse_part.1 = (f32[4,512,128]{2,1,0:T(8,128)S(1)}, f32[256,128]{1,0:T(8,128)S(1)}, f32[256,128]{1,0:T(8,128)S(1)}) custom-call(s32[4]{0:T(128)S(1)} %bitcast.19, s32[1]{0:T(128)} %bitcast.1.core, s32[1]{0:T(128)} %bitcast.2.z, bf16[4,512,256]{2,1,0:T(8,128)(2,1)S(1)} %get-tuple-element.32.turned, bf16[4,256,128]{2,1,0:T(8,128)(2,1)S(1)} %pad_maximum_fusion.ring, ...), custom_call_target="tpu_custom_call" | custom-call | tf_op jit(solution)/shard_map/coarse_part/pallas_call | solution.py:368
  75.3 0.3 collective-permute-start.6
  75.5 4.6 %collective-permute-start.7 = (f32[256,128]{1,0:T(8,128)S(1)}, f32[256,128]{1,0:T(8,128)S(1)}, u32[]{:S(2)}, u32[]{:S(2)}) collective-permute-start(f32[256,128]{1,0:T(8,128)S(1)} %get-tuple-element.39), channel_id=1, source_target_pairs={{1,0},{2,1},{3,2},{4,3},{5,4},{6,5},{7,6},{8,7},{9,8},{10,9},{11,1... | collective-permute-start | bytes 393224 | tf_op jit(solution)/shard_map/ppermute | solution.py:621
  80.1 6.2 %search_inner.1 = (f32[2,512,256]{2,1,0:T(8,128)S(1)}, f32[4,128]{1,0:T(4,128)S(1)}) custom-call(bf16[4,512,512]{2,1,0:T(8,128)(2,1)} %stiffness.3, bf16[4,512,1152]{2,1,0:T(8,128)(2,1)} %coupling.3, bf16[4,1152,1152]{2,1,0:T(8,128)(2,1)} %interior.3, f32[4,512,128]{2,1,0:T(8,128)S(1)} %get-tuple-element.37.pre, f32[4,256,128]{2,1,0:T(8,128)S(1)} %copy-done.1, ...), custom_call_target="tpu_custom_call" | custom-call | flops 2835349504 | bytes 8716288 | tf_op jit(solution)/shard_map/search_inner/pallas_call | solution.py:503
  86.3 6.3 %search_outer.1 = (f32[2,512,256]{2,1,0:T(8,128)S(1)}, f32[128,4,128]{2,1,0:T(4,128)S(1)}, f32[256,256]{1,0:T(8,128)S(1)}) custom-call(bf16[4,512,512]{2,1,0:T(8,128)(2,1)} %stiffness.3, bf16[4,512,1152]{2,1,0:T(8,128)(2,1)} %coupling.3, bf16[4,1152,1152]{2,1,0:T(8,128)(2,1)} %interior.3, f32[4,512,128]{2,1,0:T(8,128)S(1)} %get-tuple-element.37.pre, ...), custom_call_target="tpu_custom_call" | custom-call | flops 2835349504 | bytes 8716288 | tf_op jit(solution)/shard_map/search_outer/pallas_call | solution.py:521
  92.7 19.3 %all_to_all.17.sums = f32[128,4,128]{2,1,0:T(4,128)S(1)} all-to-all(f32[128,4,128]{2,1,0:T(4,128)S(1)} %get-tuple-element.42), channel_id=1, replica_groups=mesh['z'=4,'core'=2,'narrow'=16] {'z','core','narrow'}, dimensions={0} | all-to-all | bytes 524288 | tf_op jit(solution)/shard_map/all_to_all | solution.py:637
  112.1 1.3 %update.1 = (f32[4,256,128]{2,1,0:T(8,128)}, f32[4,256,128]{2,1,0:T(8,128)}) custom-call(f32[128,4,128]{2,1,0:T(4,128)S(1)} %all_to_all.17.sums, f32[1,128]{1,0:T(1,128)S(1)} %bitcast.20, f32[4,512,128]{2,1,0:T(8,128)S(1)} %get-tuple-element.37.pre, f32[256,128]{1,0:T(8,128)S(1)} %collective-permute-done.6.from_prev, ...), custom_call_target="tpu_custom_call" | custom-call | tf_op jit(solution)/shard_map/update/pallas_call | solution.py:567
  (24 shorter events, 0.3 us)
Async XLA Ops:
  1.5 9.9 %collective-permute-start = (bf16[256,128]{1,0:T(8,128)(2,1)S(1)}, bf16[256,128]{1,0:T(8,128)(2,1)S(1)}, u32[]{:S(2)}, u32[]{:S(2)}) collective-permute-start(bf16[256,128]{1,0:T(8,128)(2,1)S(1)} %fusion), channel_id=1, source_target_pairs={{1,0},{2,1},{3,2},{4,3},{5,4},{6,5},{7,6},{8,7},{9,8},{10,9},{11,1... | collective-permute-start | bytes 196616 | tf_op jit(solution)/shard_map/ppermute | solution.py:599
  7.3 4.2 %copy-start.4 = (s32[4,1]{0,1:T(1,128)S(1)}, s32[4,1]{0,1:T(1,128)}, u32[]{:S(2)}) copy-start(s32[4,1]{0,1:T(1,128)} %param.25) | copy-start | bytes 52
  12.6 3.7 %collective-permute-start.1 = (f32[4,640,128]{2,1,0:T(8,128)S(1)}, f32[4,640,128]{2,1,0:T(8,128)S(1)}, u32[]{:S(2)}, u32[]{:S(2)}) collective-permute-start(f32[4,640,128]{2,1,0:T(8,128)S(1)} %get-tuple-element.28), channel_id=1, source_target_pairs={{0,16},{16,0},{1,17},{17,1},{2,18},{18,2},{3,19},{19,3},{4,20},{20... | collective-permute-start | bytes 3932168 | tf_op jit(solution)/shard_map/ppermute | solution.py:603
  45.3 11.3 %copy-start.3 = (f32[1,256,256]{2,1,0:T(8,128)S(1)}, f32[1,256,256]{2,1,0:T(8,128)}, u32[]{:S(2)}) copy-start(f32[1,256,256]{2,1,0:T(8,128)} %base.1) | copy-start | bytes 786436
  45.3 18.7 %copy-start.1 = (f32[4,256,128]{2,1,0:T(8,128)S(1)}, f32[4,256,128]{2,1,0:T(8,128)}, u32[]{:S(2)}) copy-start(f32[4,256,128]{2,1,0:T(8,128)} %direction.5) | copy-start | bytes 1572868
  45.3 18.7 %copy-start = (f32[4,256,128]{2,1,0:T(8,128)S(1)}, f32[4,256,128]{2,1,0:T(8,128)}, u32[]{:S(2)}) copy-start(f32[4,256,128]{2,1,0:T(8,128)} %residual.5) | copy-start | bytes 1572868
  60.8 6.8 %collective-permute-start.2 = (bf16[256,128]{1,0:T(8,128)(2,1)S(1)}, bf16[256,128]{1,0:T(8,128)(2,1)S(1)}, u32[]{:S(2)}, u32[]{:S(2)}) collective-permute-start(bf16[256,128]{1,0:T(8,128)(2,1)S(1)} %solve_block.1), channel_id=1, source_target_pairs={{0,32},{32,64},{64,96},{96,0},{1,33},{33,65},{65,97},{97,1},{2,34}... | collective-permute-start | bytes 196616 | tf_op jit(solution)/shard_map/ppermute | solution.py:612
  61.0 6.6 %collective-permute-start.3 = (bf16[256,128]{1,0:T(8,128)(2,1)S(1)}, bf16[256,128]{1,0:T(8,128)(2,1)S(1)}, u32[]{:S(2)}, u32[]{:S(2)}) collective-permute-start(bf16[256,128]{1,0:T(8,128)(2,1)S(1)} %solve_block.1), channel_id=1, source_target_pairs={{0,64},{32,96},{64,0},{96,32},{1,65},{33,97},{65,1},{97,33},{2,66}... | collective-permute-start | bytes 196616 | tf_op jit(solution)/shard_map/ppermute | solution.py:612
  61.9 5.6 %collective-permute-start.4 = (bf16[256,128]{1,0:T(8,128)(2,1)S(1)}, bf16[256,128]{1,0:T(8,128)(2,1)S(1)}, u32[]{:S(2)}, u32[]{:S(2)}) collective-permute-start(bf16[256,128]{1,0:T(8,128)(2,1)S(1)} %solve_block.1), channel_id=1, source_target_pairs={{0,96},{32,0},{64,32},{96,64},{1,97},{33,1},{65,33},{97,65},{2,98}... | collective-permute-start | bytes 196616 | tf_op jit(solution)/shard_map/ppermute | solution.py:612
  67.6 5.6 %collective-permute-start.5 = (bf16[4,256,128]{2,1,0:T(8,128)(2,1)S(1)}, bf16[4,256,128]{2,1,0:T(8,128)(2,1)}, u32[]{:S(2)}, u32[]{:S(2)}) collective-permute-start(bf16[4,256,128]{2,1,0:T(8,128)(2,1)S(1)} %pad_maximum_fusion.ring), channel_id=1, source_target_pairs={{0,16},{16,0},{1,17},{17,1},{2,18},{18,2},{3,19},{19,3},{4,20},{20... | collective-permute-start | bytes 786440 | tf_op jit(solution)/shard_map/ppermute | solution.py:618
  72.0 14.3 %collective-permute-start.8 = (f32[256,128]{1,0:T(8,128)S(1)}, f32[256,128]{1,0:T(8,128)S(1)}, u32[]{:S(2)}, u32[]{:S(2)}) collective-permute-start(f32[256,128]{1,0:T(8,128)S(1)} %slice_bitcast_fusion), channel_id=1, source_target_pairs={{1,0},{2,1},{3,2},{4,3},{5,4},{6,5},{7,6},{8,7},{9,8},{10,9},{11,1... | collective-permute-start | bytes 393224 | tf_op jit(solution)/shard_map/ppermute | solution.py:614
  75.3 11.0 %collective-permute-start.6 = (f32[256,128]{1,0:T(8,128)S(1)}, f32[256,128]{1,0:T(8,128)S(1)}, u32[]{:S(2)}, u32[]{:S(2)}) collective-permute-start(f32[256,128]{1,0:T(8,128)S(1)} %get-tuple-element.38), channel_id=1, source_target_pairs={{0,1},{1,2},{2,3},{3,4},{4,5},{5,6},{6,7},{7,8},{8,9},{9,10},{10,1... | collective-permute-start | bytes 393224 | tf_op jit(solution)/shard_map/ppermute | solution.py:620
  75.5 10.8 %collective-permute-start.7 = (f32[256,128]{1,0:T(8,128)S(1)}, f32[256,128]{1,0:T(8,128)S(1)}, u32[]{:S(2)}, u32[]{:S(2)}) collective-permute-start(f32[256,128]{1,0:T(8,128)S(1)} %get-tuple-element.39), channel_id=1, source_target_pairs={{1,0},{2,1},{3,2},{4,3},{5,4},{6,5},{7,6},{8,7},{9,8},{10,9},{11,1... | collective-permute-start | bytes 393224 | tf_op jit(solution)/shard_map/ppermute | solution.py:621
  86.3 25.7 %copy-start.2 = (f32[4,256,128]{2,1,0:T(8,128)S(1)}, f32[4,256,128]{2,1,0:T(8,128)}, u32[]{:S(2)}) copy-start(f32[4,256,128]{2,1,0:T(8,128)} %solution.1) | copy-start | bytes 1572868
  86.3 25.7 %copy-start.5 = (f32[128]{0:T(128)S(1)}, f32[128]{0:T(128)}, u32[]{:S(2)}) copy-start(f32[128]{0:T(128)} %param.17) | copy-start | bytes 1540
  92.6 19.4 %collective-permute-start.9 = (f32[256,256]{1,0:T(8,128)S(1)}, f32[256,256]{1,0:T(8,128)S(1)}, u32[]{:S(2)}, u32[]{:S(2)}) collective-permute-start(f32[256,256]{1,0:T(8,128)S(1)} %get-tuple-element.45), channel_id=1, source_target_pairs={{0,1},{1,2},{2,3},{3,4},{4,5},{5,6},{6,7},{7,8},{8,9},{9,10},{10,1... | collective-permute-start | bytes 786440 | tf_op jit(solution)/shard_map/ppermute | solution.py:636

commit v4 on v3

--- a/solution.py
+++ b/solution.py
@@ -12,7 +12,6 @@
 TN = (((0,), (0,)), ((), ()))
 SMALL = 16 * 1024 * 1024
 LARGE = 24 * 1024 * 1024
-INNER = 24 * 1024 * 1024
 PLACE = 16 * 1024 * 1024
 HIGHEST = lax.Precision.HIGHEST
 
@@ -268,7 +267,7 @@
             new = column_sum(left * scaled)
             p[...] = scaled + jnp.where(norm > 0.0, new / norm, 0.0) * p[...]
             norm = new
-        return count + 2, norm, jnp.max(norm - 1e-13 * start) > 0.0
+        return count + 2, norm, jnp.max(norm - 1e-12 * start) > 0.0
 
     lax.while_loop(
         lambda state: state[2] & (state[0] < MOST_STEPS), steps, (jnp.int32(0), start, jnp.bool_(True))
@@ -303,6 +302,22 @@
         compiler_params=params(),
         name="solve_block",
     )(packed, base)
+
+
+def fetches(subs, sources, places, sems):
+    return [
+        pltpu.make_async_copy(source.at[s], place.at[j], sems.at[k, j])
+        for k, (source, place) in enumerate(zip(sources, places))
+        for j, s in enumerate(subs)
+    ]
+
+
+def fetched(operators):
+    return [jax.ShapeDtypeStruct((2,) + x.shape[1:], x.dtype) for x in operators]
+
+
+ANYWHERE = pl.BlockSpec(memory_space=pl.ANY)
+IN_HBM = pl.BlockSpec(memory_space=pltpu.HBM)
 
 
 def neumann_kernel(pm, neumann, basis, res, halo, out, turned):
@@ -399,14 +414,6 @@
     return dot(stiffness, field.astype(BF16)) - dot(coupling, inside, NT)
 
 
-def operators(nb, ni, place):
-    return [
-        pl.BlockSpec((1, nb, nb), place),
-        pl.BlockSpec((1, nb, ni), place),
-        pl.BlockSpec((1, ni, ni), place),
-    ]
-
-
 def cost(steps, nb, ni, rhs):
     return pl.CostEstimate(
         flops=2 * steps * rhs * (nb * nb + 2 * nb * ni + ni * ni),
@@ -435,14 +442,27 @@
     return both, parts
 
 
-def inner_kernel(stiffness, coupling, interior, pre, direction, residual, out, sums):
+def inner_kernel(
+    coupling, interior, stiffness, near_p, far_p, behind_p, ahead_p, own_d, far_d, own_r, *rest
+):
+    sources, (out, sums), places, sems = rest[:3], rest[3:5], rest[5:8], rest[8]
     i = pl.program_id(0)
-    s = i + 1
-    face = direction.shape[1]
-    own_p = pre[s, :face] + pre[s - 1, face:]
-    far_p = pre[s + 1, :face] + pre[s, face:]
+    copies = fetches((0, sources[0].shape[0] - 1), sources, places, sems)
+
+    @pl.when(i == 0)
+    def _():
+        for copy in copies:
+            copy.start()
+
     out[0], parts = act(
-        stiffness, coupling, interior, own_p, far_p, direction[s], direction[s + 1], residual[s]
+        stiffness,
+        coupling,
+        interior,
+        near_p[0] + behind_p[0],
+        ahead_p[0] + far_p[0],
+        own_d[0],
+        far_d[0],
+        own_r[0],
     )
 
     @pl.when(i == 0)
@@ -452,18 +472,24 @@
     @pl.when(i > 0)
     def _():
         sums[...] += parts
+        for copy in copies:
+            copy.wait()
 
 
 def outer_kernel(
-    stiffness,
     coupling,
     interior,
-    pre,
+    stiffness,
+    near_p,
+    far_p,
+    behind_p,
+    ahead_p,
+    own_d,
+    far_d,
+    own_r,
     from_prev,
     from_next,
-    direction,
     direction_halo,
-    residual,
     earlier,
     out,
     copies,
@@ -471,17 +497,11 @@
     sums,
 ):
     i = pl.program_id(0)
-    last = direction.shape[0] - 1
-    s = i * last
-    near = jnp.minimum(s + 1, last)
-    behind = jnp.maximum(s - 1, 0)
-    face = direction.shape[1]
-    own_p = pre[s, :face] + jnp.where(i == 0, from_prev[...], pre[behind, face:])
-    far_p = pre[s, face:] + jnp.where(i == 0, pre[near, :face], from_next[...])
-    far_d = jnp.where(i == 0, direction[near], direction_halo[...])
-    both, parts = act(
-        stiffness, coupling, interior, own_p, far_p, direction[s], far_d, residual[s]
-    )
+    face = far.shape[0]
+    own = near_p[0] + jnp.where(i == 0, from_prev[...], behind_p[0])
+    after = far_p[0] + jnp.where(i == 0, ahead_p[0], from_next[...])
+    after_d = jnp.where(i == 0, far_d[0], direction_halo[...])
+    both, parts = act(stiffness, coupling, interior, own, after, own_d[0], after_d, own_r[0])
     out[0] = both
 
     @pl.when(i == 0)
@@ -496,47 +516,65 @@
             copies[k] = total
 
 
-def search_inner(stiffness, coupling, interior, pre, direction, residual):
-    subs, nb, ni = coupling.shape
+def search(kernel, name, first, stride, extra, scratch, held, pre, direction, residual, *rest, ahead=()):
+    _, nb, ni = held[0].shape
+    subs = direction.shape[0]
     rhs = direction.shape[2]
-    rest = (pre, direction, residual)
+    face = nb // 2
+    last = subs - 1
+
+    def block(shape, shift=0, half=0):
+        def place(i):
+            s = first + stride * i + shift
+            return (jnp.minimum(jnp.maximum(s, 0), last), half, 0)
+
+        return pl.BlockSpec((1,) + shape, place)
+
+    def operator(shape):
+        if held[0].shape[0] == subs:
+            return block(shape)
+        return pl.BlockSpec((1,) + shape, lambda i: (i, 0, 0))
+
+    faces = (face, rhs)
     return pl.pallas_call(
-        inner_kernel,
-        grid=(subs - 2,),
-        in_specs=operators(nb, ni, lambda i: (i + 1, 0, 0)) + [whole(x.shape) for x in rest],
-        out_specs=[pl.BlockSpec((1, nb, 2 * rhs), lambda i: (i, 0, 0)), whole((4, rhs))],
-        out_shape=[
-            jax.ShapeDtypeStruct((subs - 2, nb, 2 * rhs), F32),
-            jax.ShapeDtypeStruct((4, rhs), F32),
-        ],
-        compiler_params=params(INNER),
-        cost_estimate=cost(subs - 2, nb, ni, 2 * rhs),
-        name="search_inner",
-    )(*stay(stiffness, coupling, interior), *rest)
-
-
-def search_outer(devices, stiffness, coupling, interior, *rest):
-    subs, nb, ni = coupling.shape
-    rhs = rest[0].shape[2]
-    return pl.pallas_call(
-        outer_kernel,
+        kernel,
         grid=(2,),
-        in_specs=operators(nb, ni, lambda i: ((subs - 1) * i, 0, 0)) + [whole(x.shape) for x in rest],
-        out_specs=[
-            pl.BlockSpec((1, nb, 2 * rhs), lambda i: (i, 0, 0)),
-            whole((devices, 4, rhs)),
-            whole((nb // 2, 2 * rhs)),
-        ],
-        out_shape=[
-            jax.ShapeDtypeStruct((2, nb, 2 * rhs), F32),
-            jax.ShapeDtypeStruct((devices, 4, rhs), F32),
-            jax.ShapeDtypeStruct((nb // 2, 2 * rhs), F32),
-        ],
-        scratch_shapes=[pltpu.VMEM((4, rhs), F32)],
+        in_specs=[
+            operator((nb, ni)),
+            operator((ni, ni)),
+            operator((nb, nb)),
+            block(faces),
+            block(faces, 0, 1),
+            block(faces, -1, 1),
+            block(faces, 1, 0),
+            block(faces),
+            block(faces, 1),
+            block(faces),
+        ]
+        + [whole(x.shape) for x in rest]
+        + [IN_HBM for _ in ahead],
+        out_specs=[pl.BlockSpec((1, nb, 2 * rhs), lambda i: (i, 0, 0))]
+        + [whole(x) for x in extra]
+        + [ANYWHERE for _ in ahead],
+        out_shape=[jax.ShapeDtypeStruct((2, nb, 2 * rhs), F32)]
+        + [jax.ShapeDtypeStruct(x, F32) for x in extra]
+        + fetched(ahead),
+        scratch_shapes=scratch,
         compiler_params=params(LARGE),
         cost_estimate=cost(2, nb, ni, 2 * rhs),
-        name="search_outer",
-    )(*stay(stiffness, coupling, interior), *rest)
+        name=name,
+    )(
+        *held,
+        pre,
+        pre,
+        pre,
+        pre,
+        direction,
+        direction,
+        residual,
+        *rest,
+        *stay(*ahead),
+    )
 
 
 def update_kernel(
@@ -619,18 +657,32 @@
     pre, near, far = coarse_part(own, core_ref, z_ref, turned, ring, twin, part)
     from_prev = lax.ppermute(far, "narrow", forward)
     from_next = lax.ppermute(near, "narrow", back)
-    inside, sums = search_inner(stiffness, coupling, interior, pre, direction, residual)
-    outer, sums, behind = search_outer(
-        devices,
-        stiffness,
-        coupling,
-        interior,
-        pre,
+    subs, nb, _ = coupling.shape
+    operators = (coupling, interior, stiffness)
+    mine = (pre, direction, residual)
+    inside, sums, *other = search(
+        inner_kernel,
+        "search_inner",
+        1,
+        1,
+        [(4, rhs)],
+        [pltpu.SemaphoreType.DMA((3, 2))],
+        stay(*operators),
+        *mine,
+        ahead=operators,
+    )
+    outer, sums, behind = search(
+        outer_kernel,
+        "search_outer",
+        0,
+        subs - 1,
+        [(devices, 4, rhs), (nb // 2, 2 * rhs)],
+        [pltpu.VMEM((4, rhs), F32)],
+        other,
+        *mine,
         from_prev,
         from_next,
-        direction,
         direction_halo,
-        residual,
         sums,
     )
     before = lax.ppermute(behind, "narrow", forward)

time: 114 us -> 112 us (0.982)
  Pallas kernels: 28.9 us -> 27.4 us
    pallas_call x2, Pallas kernels: 12.4 us -> 10.9 us  [search(): pl.pallas_call(kernel, grid=(2,), in_specs=[operator((nb, ni)), operator(...]
    ppermute x3, starting transfers between devices: 3.13 us -> 1.98 us  [local(): lax.ppermute(solved, 'z', [(i, (i + d) % groups) for i in range(groups)])]
  transfers between devices with their start and end apart: 10 -> 10, of which waited for: 2 -> 3; matrix products, arithmetic and copies ran while one was open for 0% -> 0% of each run, Pallas kernels for 14% -> 15%
where the time goes in v4:
time: 112 us
  blocking collectives  59 us (53%)
  Pallas kernels  27.4 us (24%)
  starting transfers between devices  20.1 us (18%)
  waiting for transfers between devices  3.62 us (3%)
    all_to_all x1, blocking collectives, local(): lax.all_to_all(mine.reshape(groups * pieces, rows, rhs), ('z', 'narrow'),...  28.8 us
    all_to_all x1, blocking collectives, local(): sums = lax.all_to_all(sums, ('z', 'core', 'narrow'), 0, 0, tiled=True)  18.9 us
    all_to_all x1, blocking collectives, local(): packed = lax.all_to_all(copies, 'narrow', 0, 0, tiled=True)  11.2 us
    pallas_call x2, Pallas kernels, search(): pl.pallas_call(kernel, grid=(2,), in_specs=[operator((nb, ni)), operator(...  10.9 us
    ppermute x1, starting transfers between devices, local(): halo = lax.ppermute(residual[0].astype(BF16), 'narrow', back)  5.76 us
    ppermute x1, starting transfers between devices, local(): twin = lax.ppermute(ring, 'core', [(0, 1), (1, 0)])  5.38 us
    ppermute x1, starting transfers between devices, local(): from_next = lax.ppermute(near, 'narrow', back)  4.6 us
    pallas_call x1, Pallas kernels, solve_block(): pl.pallas_call(solve_kernel, out_shape=jax.ShapeDtypeStruct((co, rhs), BF...  4.22 us
  transfers between devices with their start and end apart: 10, of which 3 were waited for; matrix products, arithmetic and copies ran while one was open for 0% of the time, Pallas kernels for 15%

profile of v4, /device:TPU:1, one launch (start us, length us, event | category | flops | bytes accessed | tf_op | source)
XLA Modules:
  0.0 111.9 jit_solution(1175503523284279954)
XLA Ops:
  0.6 0.9 fusion
  1.5 5.8 %collective-permute-start = (bf16[256,128]{1,0:T(8,128)(2,1)S(1)}, bf16[256,128]{1,0:T(8,128)(2,1)S(1)}, u32[]{:S(2)}, u32[]{:S(2)}) collective-permute-start(bf16[256,128]{1,0:T(8,128)(2,1)S(1)} %fusion), channel_id=1, source_target_pairs={{1,0},{2,1},{3,2},{4,3},{5,4},{6,5},{7,6},{8,7},{9,8},{10,9},{11,1... | collective-permute-start | bytes 196616 | tf_op jit(solution)/shard_map/ppermute | solution.py:637
  7.3 4.2 %place_panels.1 = (f32[4,640,128]{2,1,0:T(8,128)S(1)}, f32[4,640,128]{2,1,0:T(8,128)S(1)}, bf16[256,256]{1,0:T(8,128)(2,1)S(1)}) custom-call(s32[4]{0:T(128)} %bitcast.17, s32[4]{0:T(128)} %chg.1, s32[1]{0:T(128)} %bitcast.1.core, s32[4,200]{1,0:T(4,128)} %pm.3, bf16[4,200,512]{2,1,0:T(8,128)(2,1)} %bitcast.22, bf16[4,200,200]{2,1,0:T(8,128)(2,1)} %panel.1, ...), custom_call_target="tpu_custom_call" | custom-call | flops 1000000000 | bytes 6000000 | tf_op jit(solution)/shard_map/place_panels/pallas_call | solution.py:91
  11.5 1.1 add_halo.1
  12.6 1.0 collective-permute-start.1
  13.6 2.7 %collective-permute-done.1 = f32[4,640,128]{2,1,0:T(8,128)S(1)} collective-permute-done((f32[4,640,128]{2,1,0:T(8,128)S(1)}, f32[4,640,128]{2,1,0:T(8,128)S(1)}, u32[]{:S(2)}, u32[]{:S(2)}) %collective-permute-start.1) | collective-permute-done | bytes 1310752 | tf_op jit(solution)/shard_map/ppermute | solution.py:641
  16.3 0.1 add.3
  16.4 28.8 %all_to_all.15.parts = f32[64,40,128]{2,1,0:T(8,128)S(1)} all-to-all(f32[64,40,128]{2,1,0:T(8,128)S(1)} %bitcast.21), channel_id=1, replica_groups=mesh['z'=4,'core'=2,'narrow'=16] {'z','narrow'}, dimensions={0} | all-to-all | bytes 2621440 | tf_op jit(solution)/shard_map/all_to_all | solution.py:643
  45.4 11.2 %all_to_all.16 = f32[16,40,128]{2,1,0:T(8,128)S(1)} all-to-all(f32[16,40,128]{2,1,0:T(8,128)S(1)} %sum_copies.1), channel_id=1, replica_groups=mesh['z'=4,'core'=2,'narrow'=16] {'narrow'}, dimensions={0} | all-to-all | bytes 655360 | tf_op jit(solution)/shard_map/all_to_all | solution.py:647
  56.5 4.2 %solve_block.1 = bf16[256,128]{1,0:T(8,128)(2,1)S(1)} custom-call(f32[640,128]{1,0:T(8,128)S(1)} %bitcast.15, f32[1,256,256]{2,1,0:T(8,128)S(1)} %copy-done.3), custom_call_target="tpu_custom_call" | custom-call | tf_op jit(solution)/shard_map/solve_block/pallas_call | solution.py:292
  60.8 0.6 collective-permute-start.4
  61.4 1.4 %collective-permute-start.3 = (bf16[256,128]{1,0:T(8,128)(2,1)S(1)}, bf16[256,128]{1,0:T(8,128)(2,1)S(1)}, u32[]{:S(2)}, u32[]{:S(2)}) collective-permute-start(bf16[256,128]{1,0:T(8,128)(2,1)S(1)} %solve_block.1), channel_id=1, source_target_pairs={{0,64},{32,96},{64,0},{96,32},{1,65},{33,97},{65,1},{97,33},{2,66}... | collective-permute-start | bytes 196616 | tf_op jit(solution)/shard_map/ppermute | solution.py:650
  62.8 3.6 %neumann_half.1 = (f32[4,512,128]{2,1,0:T(8,128)S(1)}, bf16[4,512,256]{2,1,0:T(8,128)(2,1)S(1)}) custom-call(s32[4,200]{1,0:T(4,128)} %pm.3, bf16[4,512,512]{2,1,0:T(8,128)(2,1)} %neumann.1, bf16[4,200,512]{2,1,0:T(8,128)(2,1)} %bitcast.23, f32[4,256,128]{2,1,0:T(8,128)S(1)} %copy-done.1, bf16[256,128]{1,0:T(8,128)(2,1)S(1)} %collective-permute-done.halo), custom_call_target="tpu_custom_call" | custom-call | flops 268435456 | bytes 4000000 | tf_op jit(solution)/shard_map/neumann_half/pallas_call | solution.py:336
  66.4 0.7 collective-permute-done.2
  67.1 5.4 %collective-permute-start.5 = (bf16[4,256,128]{2,1,0:T(8,128)(2,1)S(1)}, bf16[4,256,128]{2,1,0:T(8,128)(2,1)}, u32[]{:S(2)}, u32[]{:S(2)}) collective-permute-start(bf16[4,256,128]{2,1,0:T(8,128)(2,1)S(1)} %pad_maximum_fusion.ring), channel_id=1, source_target_pairs={{0,16},{16,0},{1,17},{17,1},{2,18},{18,2},{3,19},{19,3},{4,20},{20... | collective-permute-start | bytes 786440 | tf_op jit(solution)/shard_map/ppermute | solution.py:656
  72.5 1.0 collective-permute-start.8
  73.5 0.3 collective-permute-done.5.twin
  73.8 2.0 %coarse_part.1 = (f32[4,512,128]{2,1,0:T(8,128)S(1)}, f32[256,128]{1,0:T(8,128)S(1)}, f32[256,128]{1,0:T(8,128)S(1)}) custom-call(s32[4]{0:T(128)S(1)} %bitcast.19, s32[1]{0:T(128)} %bitcast.1.core, s32[1]{0:T(128)} %bitcast.2.z, bf16[4,512,256]{2,1,0:T(8,128)(2,1)S(1)} %get-tuple-element.35.turned, bf16[4,256,128]{2,1,0:T(8,128)(2,1)S(1)} %pad_maximum_fusion.ring, ...), custom_call_target="tpu_custom_call" | custom-call | tf_op jit(solution)/shard_map/coarse_part/pallas_call | solution.py:383
  75.8 0.3 collective-permute-start.6
  76.1 4.6 %collective-permute-start.7 = (f32[256,128]{1,0:T(8,128)S(1)}, f32[256,128]{1,0:T(8,128)S(1)}, u32[]{:S(2)}, u32[]{:S(2)}) collective-permute-start(f32[256,128]{1,0:T(8,128)S(1)} %get-tuple-element.45), channel_id=1, source_target_pairs={{1,0},{2,1},{3,2},{4,3},{5,4},{6,5},{7,6},{8,7},{9,8},{10,9},{11,1... | collective-permute-start | bytes 393224 | tf_op jit(solution)/shard_map/ppermute | solution.py:659
  80.7 6.9 %search_inner.1 = (f32[2,512,256]{2,1,0:T(8,128)S(1)}, f32[4,128]{1,0:T(4,128)S(1)}, bf16[2,512,1152]{2,1,0:T(8,128)(2,1)S(1)}, bf16[2,1152,1152]{2,1,0:T(8,128)(2,1)S(1)}, bf16[2,512,512]{2,1,0:T(8,128)(2,1)S(1)}) custom-call(bf16[4,512,1152]{2,1,0:T(8,128)(2,1)} %rest_0_.1, bf16[4,1152,1152]{2,1,0:T(8,128)(2,1)} %rest_1_.1, bf16[4,512,512]{2,1,0:T(8,128)(2,1)} %rest_2_.1, ...), custom_call_target="tpu_custom_call" | custom-call | flops 2835349504 | bytes 8716288 | tf_op jit(solution)/shard_map/search_inner/pallas_call | solution.py:539
  87.6 4.0 %search_outer.1 = (f32[2,512,256]{2,1,0:T(8,128)S(1)}, f32[128,4,128]{2,1,0:T(4,128)S(1)}, f32[256,256]{1,0:T(8,128)S(1)}) custom-call(bf16[2,512,1152]{2,1,0:T(8,128)(2,1)S(1)} %get-tuple-element.41.coupling, bf16[2,1152,1152]{2,1,0:T(8,128)(2,1)S(1)} %get-tuple-element.42.interior, bf16[2,512,512]{2,1,0:T(8,128)(2,1)S(1)} %get-tuple-element.43.stiffness, ...), custom_call_target="tpu_custom_call" | custom-call | flops 2835349504 | bytes 8716288 | tf_op jit(solution)/shard_map/search_outer/pallas_call | solution.py:539
  91.7 18.9 %all_to_all.17.sums = f32[128,4,128]{2,1,0:T(4,128)S(1)} all-to-all(f32[128,4,128]{2,1,0:T(4,128)S(1)} %get-tuple-element.48), channel_id=1, replica_groups=mesh['z'=4,'core'=2,'narrow'=16] {'z','core','narrow'}, dimensions={0} | all-to-all | bytes 524288 | tf_op jit(solution)/shard_map/all_to_all | solution.py:689
  110.6 1.3 %update.1 = (f32[4,256,128]{2,1,0:T(8,128)}, f32[4,256,128]{2,1,0:T(8,128)}) custom-call(f32[128,4,128]{2,1,0:T(4,128)S(1)} %all_to_all.17.sums, f32[1,128]{1,0:T(1,128)S(1)} %bitcast.20, f32[4,512,128]{2,1,0:T(8,128)S(1)} %get-tuple-element.40.near_p.far_p.behind_p.ahead_p.pre, f32[256,128]{1,0:T(8,128)S(1)} %collective-permute-done.6.from_prev, ...), custom_call_target="tpu_custom_call" | custom-call | tf_op jit(solution)/shard_map/update/pallas_call | solution.py:605
  (24 shorter events, 0.3 us)
Async XLA Ops:
  1.5 9.9 %collective-permute-start = (bf16[256,128]{1,0:T(8,128)(2,1)S(1)}, bf16[256,128]{1,0:T(8,128)(2,1)S(1)}, u32[]{:S(2)}, u32[]{:S(2)}) collective-permute-start(bf16[256,128]{1,0:T(8,128)(2,1)S(1)} %fusion), channel_id=1, source_target_pairs={{1,0},{2,1},{3,2},{4,3},{5,4},{6,5},{7,6},{8,7},{9,8},{10,9},{11,1... | collective-permute-start | bytes 196616 | tf_op jit(solution)/shard_map/ppermute | solution.py:637
  7.3 4.2 %copy-start.4 = (s32[4,1]{0,1:T(1,128)S(1)}, s32[4,1]{0,1:T(1,128)}, u32[]{:S(2)}) copy-start(s32[4,1]{0,1:T(1,128)} %param.25) | copy-start | bytes 52
  12.6 3.7 %collective-permute-start.1 = (f32[4,640,128]{2,1,0:T(8,128)S(1)}, f32[4,640,128]{2,1,0:T(8,128)S(1)}, u32[]{:S(2)}, u32[]{:S(2)}) collective-permute-start(f32[4,640,128]{2,1,0:T(8,128)S(1)} %get-tuple-element.31), channel_id=1, source_target_pairs={{0,16},{16,0},{1,17},{17,1},{2,18},{18,2},{3,19},{19,3},{4,20},{20... | collective-permute-start | bytes 3932168 | tf_op jit(solution)/shard_map/ppermute | solution.py:641
  45.3 11.3 %copy-start.3 = (f32[1,256,256]{2,1,0:T(8,128)S(1)}, f32[1,256,256]{2,1,0:T(8,128)}, u32[]{:S(2)}) copy-start(f32[1,256,256]{2,1,0:T(8,128)} %base.1) | copy-start | bytes 786436
  45.3 17.5 %copy-start = (f32[4,256,128]{2,1,0:T(8,128)S(1)}, f32[4,256,128]{2,1,0:T(8,128)}, u32[]{:S(2)}) copy-start(f32[4,256,128]{2,1,0:T(8,128)} %direction.1) | copy-start | bytes 1572868
  45.3 17.5 %copy-start.1 = (f32[4,256,128]{2,1,0:T(8,128)S(1)}, f32[4,256,128]{2,1,0:T(8,128)}, u32[]{:S(2)}) copy-start(f32[4,256,128]{2,1,0:T(8,128)} %residual.1) | copy-start | bytes 1572868
  60.8 5.6 %collective-permute-start.4 = (bf16[256,128]{1,0:T(8,128)(2,1)S(1)}, bf16[256,128]{1,0:T(8,128)(2,1)S(1)}, u32[]{:S(2)}, u32[]{:S(2)}) collective-permute-start(bf16[256,128]{1,0:T(8,128)(2,1)S(1)} %solve_block.1), channel_id=1, source_target_pairs={{0,96},{32,0},{64,32},{96,64},{1,97},{33,1},{65,33},{97,65},{2,98}... | collective-permute-start | bytes 196616 | tf_op jit(solution)/shard_map/ppermute | solution.py:650
  61.4 5.0 %collective-permute-start.3 = (bf16[256,128]{1,0:T(8,128)(2,1)S(1)}, bf16[256,128]{1,0:T(8,128)(2,1)S(1)}, u32[]{:S(2)}, u32[]{:S(2)}) collective-permute-start(bf16[256,128]{1,0:T(8,128)(2,1)S(1)} %solve_block.1), channel_id=1, source_target_pairs={{0,64},{32,96},{64,0},{96,32},{1,65},{33,97},{65,1},{97,33},{2,66}... | collective-permute-start | bytes 196616 | tf_op jit(solution)/shard_map/ppermute | solution.py:650
  62.8 4.3 %collective-permute-start.2 = (bf16[256,128]{1,0:T(8,128)(2,1)S(1)}, bf16[256,128]{1,0:T(8,128)(2,1)S(1)}, u32[]{:S(2)}, u32[]{:S(2)}) collective-permute-start(bf16[256,128]{1,0:T(8,128)(2,1)S(1)} %solve_block.1), channel_id=1, source_target_pairs={{0,32},{32,64},{64,96},{96,0},{1,33},{33,65},{65,97},{97,1},{2,34}... | collective-permute-start | bytes 196616 | tf_op jit(solution)/shard_map/ppermute | solution.py:650
  67.1 6.7 %collective-permute-start.5 = (bf16[4,256,128]{2,1,0:T(8,128)(2,1)S(1)}, bf16[4,256,128]{2,1,0:T(8,128)(2,1)}, u32[]{:S(2)}, u32[]{:S(2)}) collective-permute-start(bf16[4,256,128]{2,1,0:T(8,128)(2,1)S(1)} %pad_maximum_fusion.ring), channel_id=1, source_target_pairs={{0,16},{16,0},{1,17},{17,1},{2,18},{18,2},{3,19},{19,3},{4,20},{20... | collective-permute-start | bytes 786440 | tf_op jit(solution)/shard_map/ppermute | solution.py:656
  72.5 15.1 %collective-permute-start.8 = (f32[256,128]{1,0:T(8,128)S(1)}, f32[256,128]{1,0:T(8,128)S(1)}, u32[]{:S(2)}, u32[]{:S(2)}) collective-permute-start(f32[256,128]{1,0:T(8,128)S(1)} %slice_bitcast_fusion), channel_id=1, source_target_pairs={{1,0},{2,1},{3,2},{4,3},{5,4},{6,5},{7,6},{8,7},{9,8},{10,9},{11,1... | collective-permute-start | bytes 393224 | tf_op jit(solution)/shard_map/ppermute | solution.py:652
  75.8 11.8 %collective-permute-start.6 = (f32[256,128]{1,0:T(8,128)S(1)}, f32[256,128]{1,0:T(8,128)S(1)}, u32[]{:S(2)}, u32[]{:S(2)}) collective-permute-start(f32[256,128]{1,0:T(8,128)S(1)} %get-tuple-element.44), channel_id=1, source_target_pairs={{0,1},{1,2},{2,3},{3,4},{4,5},{5,6},{6,7},{7,8},{8,9},{9,10},{10,1... | collective-permute-start | bytes 393224 | tf_op jit(solution)/shard_map/ppermute | solution.py:658
  76.1 11.5 %collective-permute-start.7 = (f32[256,128]{1,0:T(8,128)S(1)}, f32[256,128]{1,0:T(8,128)S(1)}, u32[]{:S(2)}, u32[]{:S(2)}) collective-permute-start(f32[256,128]{1,0:T(8,128)S(1)} %get-tuple-element.45), channel_id=1, source_target_pairs={{1,0},{2,1},{3,2},{4,3},{5,4},{6,5},{7,6},{8,7},{9,8},{10,9},{11,1... | collective-permute-start | bytes 393224 | tf_op jit(solution)/shard_map/ppermute | solution.py:659
  87.6 23.0 %copy-start.2 = (f32[4,256,128]{2,1,0:T(8,128)S(1)}, f32[4,256,128]{2,1,0:T(8,128)}, u32[]{:S(2)}) copy-start(f32[4,256,128]{2,1,0:T(8,128)} %solution.1) | copy-start | bytes 1572868
  87.6 23.0 %copy-start.5 = (f32[128]{0:T(128)S(1)}, f32[128]{0:T(128)}, u32[]{:S(2)}) copy-start(f32[128]{0:T(128)} %param.17) | copy-start | bytes 1540
  91.6 19.0 %collective-permute-start.9 = (f32[256,256]{1,0:T(8,128)S(1)}, f32[256,256]{1,0:T(8,128)S(1)}, u32[]{:S(2)}, u32[]{:S(2)}) collective-permute-start(f32[256,256]{1,0:T(8,128)S(1)} %get-tuple-element.51), channel_id=1, source_target_pairs={{0,1},{1,2},{2,3},{3,4},{4,5},{5,6},{6,7},{7,8},{8,9},{9,10},{10,1... | collective-permute-start | bytes 786440 | tf_op jit(solution)/shard_map/ppermute | solution.py:688

commit v5 on v4

--- a/solution.py
+++ b/solution.py
@@ -359,22 +359,24 @@
     )(*stay(prim_map, neumann, basis), residual, halo)
 
 
-def coarse_kernel(own, core, z, turned, ring, twin, part, out, near, far):
-    s = pl.program_id(0)
-    face = far.shape[0]
+def solution_of(s, own, core, z, ring, twin):
     groups = ring.shape[0]
     at = lax.rem(z[0] - (own[s] >> 1) + groups, groups)
-    solved = jnp.where((own[s] & 1) != core[0], twin[at].astype(F32), ring[at].astype(F32)).astype(BF16)
-    found = part[0] + 0.5 * dot(turned[0], solved)
-    out[0] = found
-
-    @pl.when(s == 0)
-    def _():
-        near[...] = found[:face]
-
-    @pl.when(s == pl.num_programs(0) - 1)
-    def _():
-        far[...] = found[face:]
+    other = (own[s] & 1) != core[0]
+    return jnp.where(other, twin[at].astype(F32), ring[at].astype(F32)).astype(BF16)
+
+
+def coarse_kernel(own, core, z, turned, ring, twin, part, out):
+    s = pl.program_id(0)
+    out[0] = part[0] + 0.5 * dot(turned[0], solution_of(s, own, core, z, ring, twin))
+
+
+def edge_kernel(own, core, z, turned, turned_last, ring, twin, part, part_last, near, far):
+    last = own.shape[0] - 1
+    near[...] = part[0] + 0.5 * dot(turned[0], solution_of(0, own, core, z, ring, twin))
+    far[...] = part_last[0] + 0.5 * dot(
+        turned_last[0], solution_of(last, own, core, z, ring, twin)
+    )
 
 
 def coarse_part(own, core, z, turned, ring, twin, part):
@@ -392,19 +394,37 @@
             whole(twin.shape),
             pl.BlockSpec((1, nb, rhs), lambda s: (s, 0, 0)),
         ],
-        out_specs=[
-            pl.BlockSpec((1, nb, rhs), lambda s: (s, 0, 0)),
-            whole((nb // 2, rhs)),
-            whole((nb // 2, rhs)),
-        ],
-        out_shape=[
-            jax.ShapeDtypeStruct((subs, nb, rhs), F32),
-            jax.ShapeDtypeStruct((nb // 2, rhs), F32),
-            jax.ShapeDtypeStruct((nb // 2, rhs), F32),
-        ],
+        out_specs=pl.BlockSpec((1, nb, rhs), lambda s: (s, 0, 0)),
+        out_shape=jax.ShapeDtypeStruct((subs, nb, rhs), F32),
         compiler_params=params(),
         name="coarse_part",
     )(own, core, z, turned, ring, twin, part)
+
+
+def coarse_edges(own, core, z, turned, ring, twin, part):
+    subs, nb, co = turned.shape
+    rhs = ring.shape[2]
+    face = nb // 2
+    shape = jax.ShapeDtypeStruct((face, rhs), F32)
+    return pl.pallas_call(
+        edge_kernel,
+        grid=(1,),
+        in_specs=[
+            smem(),
+            smem(),
+            smem(),
+            pl.BlockSpec((1, face, co), lambda _: (0, 0, 0)),
+            pl.BlockSpec((1, face, co), lambda _: (subs - 1, 1, 0)),
+            whole(ring.shape),
+            whole(twin.shape),
+            pl.BlockSpec((1, face, rhs), lambda _: (0, 0, 0)),
+            pl.BlockSpec((1, face, rhs), lambda _: (subs - 1, 1, 0)),
+        ],
+        out_specs=[whole((face, rhs)), whole((face, rhs))],
+        out_shape=[shape, shape],
+        compiler_params=params(),
+        name="coarse_edges",
+    )(own, core, z, turned, turned, ring, twin, part, part)
 
 
 def action(stiffness, coupling, interior, field):
@@ -654,9 +674,11 @@
     turns, part, turned = lax.optimization_barrier((turns, part, turned))
     ring = jnp.stack([solved] + turns)
     twin = lax.ppermute(ring, "core", [(0, 1), (1, 0)])
-    pre, near, far = coarse_part(own, core_ref, z_ref, turned, ring, twin, part)
+    near, far = coarse_edges(own, core_ref, z_ref, turned, ring, twin, part)
     from_prev = lax.ppermute(far, "narrow", forward)
     from_next = lax.ppermute(near, "narrow", back)
+    part, _, _ = lax.optimization_barrier((part, near, far))
+    pre = coarse_part(own, core_ref, z_ref, turned, ring, twin, part)
     subs, nb, _ = coupling.shape
     operators = (coupling, interior, stiffness)
     mine = (pre, direction, residual)

time: 112 us -> 111 us (level)
  starting transfers between devices: 20.1 us -> 17 us
    ppermute x1, starting transfers between devices: 4.6 us -> 1.09 us  [local(): from_next = lax.ppermute(near, 'narrow', back)]
    pallas_call x0 -> x1, Pallas kernels: none -> 1.19 us  [coarse_edges(): pl.pallas_call(edge_kernel, grid=(1,), in_specs=[smem(), smem(), smem(),...]
  transfers between devices with their start and end apart: 10 -> 10, of which waited for: 3 -> 3; matrix products, arithmetic and copies ran while one was open for 0% -> 0% of each run, Pallas kernels for 15% -> 16%
where the time goes in v5:
time: 111 us
  blocking collectives  59.5 us (54%)
  Pallas kernels  28.5 us (26%)
  starting transfers between devices  17 us (15%)
  waiting for transfers between devices  3.62 us (3%)
    all_to_all x1, blocking collectives, local(): lax.all_to_all(mine.reshape(groups * pieces, rows, rhs), ('z', 'narrow'),...  28.8 us
    all_to_all x1, blocking collectives, local(): sums = lax.all_to_all(sums, ('z', 'core', 'narrow'), 0, 0, tiled=True)  19.5 us
    all_to_all x1, blocking collectives, local(): packed = lax.all_to_all(copies, 'narrow', 0, 0, tiled=True)  11.2 us
    pallas_call x2, Pallas kernels, search(): pl.pallas_call(kernel, grid=(2,), in_specs=[operator((nb, ni)), operator(...  10.9 us
    ppermute x1, starting transfers between devices, local(): halo = lax.ppermute(residual[0].astype(BF16), 'narrow', back)  5.76 us
    ppermute x1, starting transfers between devices, local(): twin = lax.ppermute(ring, 'core', [(0, 1), (1, 0)])  5.38 us
    pallas_call x1, Pallas kernels, solve_block(): pl.pallas_call(solve_kernel, out_shape=jax.ShapeDtypeStruct((co, rhs), BF...  4.22 us
    pallas_call x1, Pallas kernels, place_panels(): pl.pallas_call(place_kernel, grid=(subs,), in_specs=[smem(), smem(), smem...  4.17 us
  transfers between devices with their start and end apart: 10, of which 3 were waited for; matrix products, arithmetic and copies ran while one was open for 0% of the time, Pallas kernels for 16%

profile of v5, /device:TPU:1, one launch (start us, length us, event | category | flops | bytes accessed | tf_op | source)
XLA Modules:
  0.0 110.6 jit_solution(4059356552684227892)
XLA Ops:
  0.6 0.9 fusion
  1.5 5.8 %collective-permute-start = (bf16[256,128]{1,0:T(8,128)(2,1)S(1)}, bf16[256,128]{1,0:T(8,128)(2,1)S(1)}, u32[]{:S(2)}, u32[]{:S(2)}) collective-permute-start(bf16[256,128]{1,0:T(8,128)(2,1)S(1)} %fusion), channel_id=1, source_target_pairs={{1,0},{2,1},{3,2},{4,3},{5,4},{6,5},{7,6},{8,7},{9,8},{10,9},{11,1... | collective-permute-start | bytes 196616 | tf_op jit(solution)/shard_map/ppermute | solution.py:657
  7.3 4.2 %place_panels.1 = (f32[4,640,128]{2,1,0:T(8,128)S(1)}, f32[4,640,128]{2,1,0:T(8,128)S(1)}, bf16[256,256]{1,0:T(8,128)(2,1)S(1)}) custom-call(s32[4]{0:T(128)} %bitcast.17, s32[4]{0:T(128)} %chg.1, s32[1]{0:T(128)} %bitcast.1.core, s32[4,200]{1,0:T(4,128)} %pm.3, bf16[4,200,512]{2,1,0:T(8,128)(2,1)} %bitcast.23, bf16[4,200,200]{2,1,0:T(8,128)(2,1)} %panel.1, ...), custom_call_target="tpu_custom_call" | custom-call | flops 1000000000 | bytes 6000000 | tf_op jit(solution)/shard_map/place_panels/pallas_call | solution.py:91
  11.5 1.1 add_halo.1
  12.6 1.0 collective-permute-start.1
  13.6 2.7 %collective-permute-done.1 = f32[4,640,128]{2,1,0:T(8,128)S(1)} collective-permute-done((f32[4,640,128]{2,1,0:T(8,128)S(1)}, f32[4,640,128]{2,1,0:T(8,128)S(1)}, u32[]{:S(2)}, u32[]{:S(2)}) %collective-permute-start.1) | collective-permute-done | bytes 1310752 | tf_op jit(solution)/shard_map/ppermute | solution.py:661
  16.4 28.8 %all_to_all.15.parts = f32[64,40,128]{2,1,0:T(8,128)S(1)} all-to-all(f32[64,40,128]{2,1,0:T(8,128)S(1)} %bitcast.22), channel_id=1, replica_groups=mesh['z'=4,'core'=2,'narrow'=16] {'z','narrow'}, dimensions={0} | all-to-all | bytes 2621440 | tf_op jit(solution)/shard_map/all_to_all | solution.py:663
  45.4 11.2 %all_to_all.16 = f32[16,40,128]{2,1,0:T(8,128)S(1)} all-to-all(f32[16,40,128]{2,1,0:T(8,128)S(1)} %sum_copies.1), channel_id=1, replica_groups=mesh['z'=4,'core'=2,'narrow'=16] {'narrow'}, dimensions={0} | all-to-all | bytes 655360 | tf_op jit(solution)/shard_map/all_to_all | solution.py:667
  56.5 4.2 %solve_block.1 = bf16[256,128]{1,0:T(8,128)(2,1)S(1)} custom-call(f32[640,128]{1,0:T(8,128)S(1)} %bitcast.15, f32[1,256,256]{2,1,0:T(8,128)S(1)} %copy-done.3), custom_call_target="tpu_custom_call" | custom-call | tf_op jit(solution)/shard_map/solve_block/pallas_call | solution.py:292
  60.8 0.6 collective-permute-start.4
  61.4 1.4 %collective-permute-start.3 = (bf16[256,128]{1,0:T(8,128)(2,1)S(1)}, bf16[256,128]{1,0:T(8,128)(2,1)S(1)}, u32[]{:S(2)}, u32[]{:S(2)}) collective-permute-start(bf16[256,128]{1,0:T(8,128)(2,1)S(1)} %solve_block.1), channel_id=1, source_target_pairs={{0,64},{32,96},{64,0},{96,32},{1,65},{33,97},{65,1},{97,33},{2,66}... | collective-permute-start | bytes 196616 | tf_op jit(solution)/shard_map/ppermute | solution.py:670
  62.8 3.6 %neumann_half.1 = (f32[4,512,128]{2,1,0:T(8,128)S(1)}, bf16[4,512,256]{2,1,0:T(8,128)(2,1)S(1)}) custom-call(s32[4,200]{1,0:T(4,128)} %pm.3, bf16[4,512,512]{2,1,0:T(8,128)(2,1)} %neumann.1, bf16[4,200,512]{2,1,0:T(8,128)(2,1)} %bitcast.24, f32[4,256,128]{2,1,0:T(8,128)S(1)} %copy-done.1, bf16[256,128]{1,0:T(8,128)(2,1)S(1)} %collective-permute-done.halo), custom_call_target="tpu_custom_call" | custom-call | flops 268435456 | bytes 4000000 | tf_op jit(solution)/shard_map/neumann_half/pallas_call | solution.py:336
  66.4 0.7 collective-permute-done.2
  67.1 5.4 %collective-permute-start.5 = (bf16[4,256,128]{2,1,0:T(8,128)(2,1)S(1)}, bf16[4,256,128]{2,1,0:T(8,128)(2,1)}, u32[]{:S(2)}, u32[]{:S(2)}) collective-permute-start(bf16[4,256,128]{2,1,0:T(8,128)(2,1)S(1)} %pad_maximum_fusion.ring), channel_id=1, source_target_pairs={{0,16},{16,0},{1,17},{17,1},{2,18},{18,2},{3,19},{19,3},{4,20},{20... | collective-permute-start | bytes 786440 | tf_op jit(solution)/shard_map/ppermute | solution.py:676
  72.5 1.0 collective-permute-start.8
  73.8 1.2 %coarse_edges.1 = (f32[256,128]{1,0:T(8,128)S(1)}, f32[256,128]{1,0:T(8,128)S(1)}) custom-call(s32[4]{0:T(128)S(1)} %bitcast.19, s32[1]{0:T(128)} %bitcast.1.core, s32[1]{0:T(128)} %bitcast.2.z, bf16[4,512,256]{2,1,0:T(8,128)(2,1)S(1)} %get-tuple-element.35.turned.turned_last, bf16[4,512,256]{2,1,0:T(8,128)(2,1)S(1)} %get-tuple-element.35.turned.turned_last, ...), custom_call_target="tpu_custom_call" | custom-call | tf_op jit(solution)/shard_map/coarse_edges/pallas_call | solution.py:409
  75.0 1.1 collective-permute-start.7
  76.1 0.4 collective-permute-start.6
  76.5 2.0 %coarse_part.1.near_p.far_p.behind_p.ahead_p.pre = f32[4,512,128]{2,1,0:T(8,128)S(1)} custom-call(s32[4]{0:T(128)S(1)} %bitcast.20, s32[1]{0:T(128)} %bitcast.1.core, s32[1]{0:T(128)} %bitcast.2.z, bf16[4,512,256]{2,1,0:T(8,128)(2,1)S(1)} %get-tuple-element.35.turned.turned_last, bf16[4,256,128]{2,1,0:T(8,128)(2,1)S(1)} %pad_maximum_fusion.ring, ...), custom_call_target="tpu_custom_call" | custom-call | tf_op jit(solution)/shard_map/coarse_part/pallas_call | solution.py:385
  78.5 6.9 %search_inner.1 = (f32[2,512,256]{2,1,0:T(8,128)S(1)}, f32[4,128]{1,0:T(4,128)S(1)}, bf16[2,512,1152]{2,1,0:T(8,128)(2,1)S(1)}, bf16[2,1152,1152]{2,1,0:T(8,128)(2,1)S(1)}, bf16[2,512,512]{2,1,0:T(8,128)(2,1)S(1)}) custom-call(bf16[4,512,1152]{2,1,0:T(8,128)(2,1)} %rest_0_.1, bf16[4,1152,1152]{2,1,0:T(8,128)(2,1)} %rest_1_.1, bf16[4,512,512]{2,1,0:T(8,128)(2,1)} %rest_2_.1, ...), custom_call_target="tpu_custom_call" | custom-call | flops 2835349504 | bytes 8716288 | tf_op jit(solution)/shard_map/search_inner/pallas_call | solution.py:559
  85.5 4.0 %search_outer.1 = (f32[2,512,256]{2,1,0:T(8,128)S(1)}, f32[128,4,128]{2,1,0:T(4,128)S(1)}, f32[256,256]{1,0:T(8,128)S(1)}) custom-call(bf16[2,512,1152]{2,1,0:T(8,128)(2,1)S(1)} %get-tuple-element.43.coupling, bf16[2,1152,1152]{2,1,0:T(8,128)(2,1)S(1)} %get-tuple-element.44.interior, bf16[2,512,512]{2,1,0:T(8,128)(2,1)S(1)} %get-tuple-element.45.stiffness, ...), custom_call_target="tpu_custom_call" | custom-call | flops 2835349504 | bytes 8716288 | tf_op jit(solution)/shard_map/search_outer/pallas_call | solution.py:559
  89.5 0.3 collective-permute-start.9
  89.7 19.5 %all_to_all.17.sums = f32[128,4,128]{2,1,0:T(4,128)S(1)} all-to-all(f32[128,4,128]{2,1,0:T(4,128)S(1)} %get-tuple-element.48), channel_id=1, replica_groups=mesh['z'=4,'core'=2,'narrow'=16] {'z','core','narrow'}, dimensions={0} | all-to-all | bytes 524288 | tf_op jit(solution)/shard_map/all_to_all | solution.py:711
  109.2 1.3 %update.1 = (f32[4,256,128]{2,1,0:T(8,128)}, f32[4,256,128]{2,1,0:T(8,128)}) custom-call(f32[128,4,128]{2,1,0:T(4,128)S(1)} %all_to_all.17.sums, f32[1,128]{1,0:T(1,128)S(1)} %bitcast.21, f32[4,512,128]{2,1,0:T(8,128)S(1)} %coarse_part.1.near_p.far_p.behind_p.ahead_p.pre, f32[256,128]{1,0:T(8,128)S(1)} %collective-permute-done.6.from_prev, ...), custom_call_target="tpu_custom_call" | custom-call | tf_op jit(solution)/shard_map/update/pallas_call | solution.py:625
  (25 shorter events, 0.6 us)
Async XLA Ops:
  1.5 9.9 %collective-permute-start = (bf16[256,128]{1,0:T(8,128)(2,1)S(1)}, bf16[256,128]{1,0:T(8,128)(2,1)S(1)}, u32[]{:S(2)}, u32[]{:S(2)}) collective-permute-start(bf16[256,128]{1,0:T(8,128)(2,1)S(1)} %fusion), channel_id=1, source_target_pairs={{1,0},{2,1},{3,2},{4,3},{5,4},{6,5},{7,6},{8,7},{9,8},{10,9},{11,1... | collective-permute-start | bytes 196616 | tf_op jit(solution)/shard_map/ppermute | solution.py:657
  7.3 4.2 %copy-start.4 = (s32[4,1]{0,1:T(1,128)S(1)}, s32[4,1]{0,1:T(1,128)}, u32[]{:S(2)}) copy-start(s32[4,1]{0,1:T(1,128)} %param.25) | copy-start | bytes 52
  12.6 3.7 %collective-permute-start.1 = (f32[4,640,128]{2,1,0:T(8,128)S(1)}, f32[4,640,128]{2,1,0:T(8,128)S(1)}, u32[]{:S(2)}, u32[]{:S(2)}) collective-permute-start(f32[4,640,128]{2,1,0:T(8,128)S(1)} %get-tuple-element.31), channel_id=1, source_target_pairs={{0,16},{16,0},{1,17},{17,1},{2,18},{18,2},{3,19},{19,3},{4,20},{20... | collective-permute-start | bytes 3932168 | tf_op jit(solution)/shard_map/ppermute | solution.py:661
  45.3 11.3 %copy-start.3 = (f32[1,256,256]{2,1,0:T(8,128)S(1)}, f32[1,256,256]{2,1,0:T(8,128)}, u32[]{:S(2)}) copy-start(f32[1,256,256]{2,1,0:T(8,128)} %base.1) | copy-start | bytes 786436
  45.3 17.5 %copy-start = (f32[4,256,128]{2,1,0:T(8,128)S(1)}, f32[4,256,128]{2,1,0:T(8,128)}, u32[]{:S(2)}) copy-start(f32[4,256,128]{2,1,0:T(8,128)} %direction.1) | copy-start | bytes 1572868
  45.3 17.5 %copy-start.1 = (f32[4,256,128]{2,1,0:T(8,128)S(1)}, f32[4,256,128]{2,1,0:T(8,128)}, u32[]{:S(2)}) copy-start(f32[4,256,128]{2,1,0:T(8,128)} %residual.1) | copy-start | bytes 1572868
  60.8 5.6 %collective-permute-start.4 = (bf16[256,128]{1,0:T(8,128)(2,1)S(1)}, bf16[256,128]{1,0:T(8,128)(2,1)S(1)}, u32[]{:S(2)}, u32[]{:S(2)}) collective-permute-start(bf16[256,128]{1,0:T(8,128)(2,1)S(1)} %solve_block.1), channel_id=1, source_target_pairs={{0,96},{32,0},{64,32},{96,64},{1,97},{33,1},{65,33},{97,65},{2,98}... | collective-permute-start | bytes 196616 | tf_op jit(solution)/shard_map/ppermute | solution.py:670
  61.4 5.0 %collective-permute-start.3 = (bf16[256,128]{1,0:T(8,128)(2,1)S(1)}, bf16[256,128]{1,0:T(8,128)(2,1)S(1)}, u32[]{:S(2)}, u32[]{:S(2)}) collective-permute-start(bf16[256,128]{1,0:T(8,128)(2,1)S(1)} %solve_block.1), channel_id=1, source_target_pairs={{0,64},{32,96},{64,0},{96,32},{1,65},{33,97},{65,1},{97,33},{2,66}... | collective-permute-start | bytes 196616 | tf_op jit(solution)/shard_map/ppermute | solution.py:670
  62.8 4.3 %collective-permute-start.2 = (bf16[256,128]{1,0:T(8,128)(2,1)S(1)}, bf16[256,128]{1,0:T(8,128)(2,1)S(1)}, u32[]{:S(2)}, u32[]{:S(2)}) collective-permute-start(bf16[256,128]{1,0:T(8,128)(2,1)S(1)} %solve_block.1), channel_id=1, source_target_pairs={{0,32},{32,64},{64,96},{96,0},{1,33},{33,65},{65,97},{97,1},{2,34}... | collective-permute-start | bytes 196616 | tf_op jit(solution)/shard_map/ppermute | solution.py:670
  67.1 6.7 %collective-permute-start.5 = (bf16[4,256,128]{2,1,0:T(8,128)(2,1)S(1)}, bf16[4,256,128]{2,1,0:T(8,128)(2,1)}, u32[]{:S(2)}, u32[]{:S(2)}) collective-permute-start(bf16[4,256,128]{2,1,0:T(8,128)(2,1)S(1)} %pad_maximum_fusion.ring), channel_id=1, source_target_pairs={{0,16},{16,0},{1,17},{17,1},{2,18},{18,2},{3,19},{19,3},{4,20},{20... | collective-permute-start | bytes 786440 | tf_op jit(solution)/shard_map/ppermute | solution.py:676
  72.5 12.9 %collective-permute-start.8 = (f32[256,128]{1,0:T(8,128)S(1)}, f32[256,128]{1,0:T(8,128)S(1)}, u32[]{:S(2)}, u32[]{:S(2)}) collective-permute-start(f32[256,128]{1,0:T(8,128)S(1)} %slice_bitcast_fusion), channel_id=1, source_target_pairs={{1,0},{2,1},{3,2},{4,3},{5,4},{6,5},{7,6},{8,7},{9,8},{10,9},{11,1... | collective-permute-start | bytes 393224 | tf_op jit(solution)/shard_map/ppermute | solution.py:672
  75.0 10.5 %collective-permute-start.7 = (f32[256,128]{1,0:T(8,128)S(1)}, f32[256,128]{1,0:T(8,128)S(1)}, u32[]{:S(2)}, u32[]{:S(2)}) collective-permute-start(f32[256,128]{1,0:T(8,128)S(1)} %get-tuple-element.40), channel_id=1, source_target_pairs={{1,0},{2,1},{3,2},{4,3},{5,4},{6,5},{7,6},{8,7},{9,8},{10,9},{11,1... | collective-permute-start | bytes 393224 | tf_op jit(solution)/shard_map/ppermute | solution.py:679
  76.1 9.4 %collective-permute-start.6 = (f32[256,128]{1,0:T(8,128)S(1)}, f32[256,128]{1,0:T(8,128)S(1)}, u32[]{:S(2)}, u32[]{:S(2)}) collective-permute-start(f32[256,128]{1,0:T(8,128)S(1)} %get-tuple-element.41), channel_id=1, source_target_pairs={{0,1},{1,2},{2,3},{3,4},{4,5},{5,6},{6,7},{7,8},{8,9},{9,10},{10,1... | collective-permute-start | bytes 393224 | tf_op jit(solution)/shard_map/ppermute | solution.py:678
  85.5 23.8 %copy-start.2 = (f32[4,256,128]{2,1,0:T(8,128)S(1)}, f32[4,256,128]{2,1,0:T(8,128)}, u32[]{:S(2)}) copy-start(f32[4,256,128]{2,1,0:T(8,128)} %solution.1) | copy-start | bytes 1572868
  85.5 23.8 %copy-start.5 = (f32[128]{0:T(128)S(1)}, f32[128]{0:T(128)}, u32[]{:S(2)}) copy-start(f32[128]{0:T(128)} %param.17) | copy-start | bytes 1540
  89.5 19.8 %collective-permute-start.9 = (f32[256,256]{1,0:T(8,128)S(1)}, f32[256,256]{1,0:T(8,128)S(1)}, u32[]{:S(2)}, u32[]{:S(2)}) collective-permute-start(f32[256,256]{1,0:T(8,128)S(1)} %get-tuple-element.51), channel_id=1, source_target_pairs={{0,1},{1,2},{2,3},{3,4},{4,5},{5,6},{6,7},{7,8},{8,9},{9,10},{10,1... | collective-permute-start | bytes 786440 | tf_op jit(solution)/shard_map/ppermute | solution.py:710
